TPU v7x, 128 devices: a whole 4x4x4 slice. The times are simulated.
128 devices in a mesh: oct: 128 (over z, y, x, core).
Axes of the slice: x: 4, y: 4, z: 4, core: 2. Of those that a mesh axis runs over, the one named last changes fastest.
Arguments:
- points: float32 [8192, 3, 128], P('oct'), may hold values from -6 to 6
- dens: float32 [8192, 32, 128], P('oct'), may hold values from -6 to 6
- surface: float32 [8192, 3, 152], P('oct'), may hold values from -6 to 6
- counts: int32 [8192], P('oct'), may hold values from 1 to 128, as said below
- ulist: int32 [8192, 27], P('oct'), may hold values from -1 to 8191, as said below
- vlist: int32 [1024, 316], P('oct'), may hold values from -1 to 1023, as said below
- up_inverse: float32 [152, 152], replicated, may hold values from -0.5 to 0.5
- down_inverse: float32 [152, 152], replicated, may hold values from -0.5 to 0.5
- shift_up: float32 [8, 152, 152], replicated, may hold values from -0.15625 to 0.15625
- shift_down: float32 [8, 152, 152], replicated, may hold values from -0.5 to 0.5
- coarse: float32 [8, 152, 152], replicated, may hold values from -0.25 to 0.25
- translate: bfloat16 [316, 152, 152], replicated, may hold values from -0.0390625 to 0.0390625
Outputs:
- potential: float32 [8192, 32, 128], P('oct')
Inputs may be any that keep to these rules, and one draw needn't show every extreme that they name: `counts`: each leaf has 1 to 128 stations in use; the first leaf of every slab of 64 leaves is full. `ulist`: slot 0 holds the leaf itself; slots 1 to 8 hold -1 or leaves of the next lower slab of 64 leaves, slots 9 to 17 -1 or leaves of the leaf's own slab, slots 18 to 26 -1 or leaves of the next upper slab. `vlist`: every id is -1 or a node of the same slab of 8 nodes or of an adjacent one.
All inputs are finite; a program needn't handle non-finite values.
Results may differ from a plain program's by a relative error of at most 0.0017.
Values may be sent and summed in bfloat16 or wider, within the bound.
A program may use at most 192 MiB of HBM per device.

v0:
```python
import jax
import jax.numpy as jnp
from jax import lax
from jax.sharding import PartitionSpec as P

HIGHEST = lax.Precision.HIGHEST


def extended(value, sides, width):
    for axis, dim in sides:
        count, length = (lax.axis_size(axis), value.shape[dim])
        up = [(i, (i + 1) % count) for i in range(count - 1)]
        down = [(j, i) for i, j in up]
        last = lax.slice_in_dim(value, length - width, length, axis=dim)
        first = lax.slice_in_dim(value, 0, width, axis=dim)
        before = lax.ppermute(last, axis, up)
        after = lax.ppermute(first, axis, down)
        value = jnp.concatenate([before, value, after], axis=dim)
    return value


def swapped(value, axis, bit):
    mask = 2**bit
    pairs = [(source, source ^ mask) for source in range(lax.axis_size(axis))]
    return lax.ppermute(value, axis, pairs)


def kernel(left_pts, right_pts):
    total_sq = jnp.zeros((left_pts.shape[1], right_pts.shape[1]), jnp.float32)
    for coord_index in range(3):
        offset = left_pts[coord_index][:, None] - right_pts[coord_index][None, :]
        total_sq = total_sq + offset * offset
    return jnp.exp(-0.5 * total_sq)


def near_field(target_pts, target_ids, source_base, flat_sources, q_width):
    source_count = flat_sources.shape[0]
    p_width = target_pts.shape[2]
    coord_len = 3 * p_width
    local_ids = target_ids - source_base
    usable = (target_ids >= 0) & (local_ids >= 0) & (local_ids < source_count)
    safe_ids = jnp.clip(local_ids, 0, source_count - 1)

    def one_leaf(leaf_pts, leaf_ids, leaf_usable):
        picked = flat_sources[leaf_ids]
        slot_count = picked.shape[0]
        src_pts = picked[:, :coord_len].reshape(slot_count, 3, p_width)
        weights = jnp.where(leaf_usable[:, None], picked[:, coord_len:], 0.0).reshape(
            slot_count, q_width, p_width
        )
        kernels = jax.vmap(kernel, in_axes=(0, None))(src_pts, leaf_pts)
        partial_sums = jnp.einsum(
            "sqp,spt->sqt", weights, kernels, precision=HIGHEST, preferred_element_type=jnp.float32
        )
        return jnp.sum(partial_sums, axis=0)

    def block_fn(block):
        return jax.vmap(one_leaf)(block[0], block[1], block[2])

    leaf_count = target_pts.shape[0]
    blocked = (
        target_pts.reshape((leaf_count // 4, 4) + target_pts.shape[1:]),
        safe_ids.reshape(leaf_count // 4, 4, -1),
        usable.reshape(leaf_count // 4, 4, -1),
    )
    result = lax.map(block_fn, blocked)
    return result.reshape(leaf_count, q_width, p_width)


def local(
    points,
    dens,
    surface,
    counts,
    ulist,
    vlist,
    up_inverse,
    down_inverse,
    shift_up,
    shift_down,
    coarse,
    translate,
):
    leaf_count, q_width, p_width = dens.shape
    eq_width = surface.shape[2]
    node_count = vlist.shape[0]
    index = lax.axis_index("oct")
    slots = jnp.arange(p_width)
    mask = (slots[None, :] < counts[:, None]).astype(jnp.float32)[:, None, :]
    masked = dens * mask
    own_sources = jnp.concatenate(
        [points.reshape(leaf_count, 3 * p_width), masked.reshape(leaf_count, q_width * p_width)],
        axis=1,
    )
    up_kernel = jax.vmap(kernel)(points, surface)
    check = jnp.einsum("lqp,lpe->lqe", masked, up_kernel, precision=HIGHEST)
    leaf_eq = jnp.dot(
        check.reshape(-1, eq_width),
        up_inverse,
        precision=HIGHEST,
        preferred_element_type=jnp.float32,
    ).reshape(leaf_count, q_width, eq_width)
    node_eq = jnp.einsum(
        "ncqe,cef->nqf", leaf_eq.reshape(-1, 8, q_width, eq_width), shift_up, precision=HIGHEST
    )
    node_send = node_eq.astype(jnp.bfloat16).reshape(node_count, q_width * eq_width)
    slab_eq = jnp.einsum("cqe,cef->qf", node_eq, shift_up, precision=HIGHEST)
    cycle = extended(node_send, (("oct", 0),), node_count)
    bit_count = lax.axis_size("oct").bit_length() - 1
    slab_local = jnp.zeros((q_width, eq_width), jnp.float32)
    current = slab_eq
    for level_start in range(0, bit_count, 3):
        width_bits = min(3, bit_count - level_start)
        child_slot = jnp.right_shift(index, level_start) & 7
        current = jnp.dot(
            current, shift_up[child_slot], precision=HIGHEST, preferred_element_type=jnp.float32
        )
        for bit_number in range(level_start, level_start + width_bits):
            current = current + swapped(current, "oct", bit_number)
        slab_local = slab_local + jnp.dot(
            current, coarse[child_slot], precision=HIGHEST, preferred_element_type=jnp.float32
        )
    cycle_rows = 3 * node_count
    cycle_view = cycle.reshape(cycle_rows, q_width, eq_width)
    cycle_base = (index - 1) * node_count
    local_ids = vlist - cycle_base
    usable = (vlist >= 0) & (local_ids >= 0) & (local_ids < cycle_rows)
    row_ids = jnp.arange(cycle_rows)
    type_block = translate.shape[0] // 4
    far_node = jnp.zeros((node_count * q_width, eq_width), jnp.float32)
    for block_index in range(4):
        lower_type = block_index * type_block
        block_ids = local_ids[:, lower_type : lower_type + type_block]
        block_usable = usable[:, lower_type : lower_type + type_block]
        selector = (
            (block_ids[:, :, None] == row_ids[None, None, :]) & block_usable[:, :, None]
        ).astype(jnp.bfloat16)
        picked = jnp.einsum(
            "ntm,mqe->nqte", selector, cycle_view, preferred_element_type=jnp.float32
        ).astype(jnp.bfloat16)
        picked = picked.reshape(node_count * q_width, type_block * eq_width)
        block_table = translate[lower_type : lower_type + type_block].reshape(
            type_block * eq_width, eq_width
        )
        far_node = far_node + jnp.dot(picked, block_table, preferred_element_type=jnp.float32)
    far_node = far_node.reshape(node_count, q_width, eq_width)
    parent_part = jnp.einsum("qe,cef->cqf", slab_local, shift_down, precision=HIGHEST)
    node_local = far_node + parent_part
    leaf_local = jnp.einsum("nqe,cef->ncqf", node_local, shift_down, precision=HIGHEST).reshape(
        leaf_count, q_width, eq_width
    )
    leaf_down = jnp.dot(
        leaf_local.reshape(-1, eq_width),
        down_inverse,
        precision=HIGHEST,
        preferred_element_type=jnp.float32,
    ).reshape(leaf_count, q_width, eq_width)
    far_pot = jnp.einsum("lqe,lpe->lqp", leaf_down, up_kernel, precision=HIGHEST)
    sources = extended(own_sources, (("oct", 0),), leaf_count)
    near_total = near_field(points, ulist, (index - 1) * leaf_count, sources, q_width)
    return (far_pot + near_total) * mask


def solution(mesh):
    placed = (
        P("oct", None, None),
        P("oct", None, None),
        P("oct", None, None),
        P("oct"),
        P("oct", None),
        P("oct", None),
        P(),
        P(),
        P(),
        P(),
        P(),
        P(),
    )
    return jax.shard_map(
        local, mesh=mesh, in_specs=placed, out_specs=P("oct", None, None), check_vma=False
    )
```

profile of v0, /device:TPU:6, one launch (start us, length us, event | category | flops | bytes accessed | tf_op | source)
XLA Modules:
  0.0 816.1 jit_solution(17492066853107991847)
XLA Ops:
  4.1 14.7 %fusion.14 = f32[64,32,152]{2,1,0:T(8,128)S(1)} fusion(f32[64,32,128]{2,1,0:T(8,128)S(1)} %broadcast_multiply_fusion, f32[64,152]{1,0:T(8,128)S(1)} %get-tuple-element.67, f32[64,128]{1,0:T(8,128)S(1)} %get-tuple-element.70, f32[64,152]{1,0:T(8,128)S(1)} %get-tuple-element.68, f32[64,128]{1,0:T(8,128)S(1)} %get-tuple-element.71, ...), kind=kOutput, calls=%fused_computation.21 | convolution fusion | flops 489357312 | bytes 2508800 | tf_op jit(solution)/shard_map/lqp,lpe->lqe/dot_general | solution.py:96
  40.8 22.3 %fusion.101 = (bf16[79,152,152]{0,2,1:T(8,128)(2,1)}, bf16[79,152,152]{0,2,1:T(8,128)(2,1)}, bf16[79,152,152]{0,2,1:T(8,128)(2,1)}, bf16[79,152,152]{0,2,1:T(8,128)(2,1)}) fusion(bf16[316,152,152]{0,2,1:T(8,128)(2,1)} %param.25), kind=kLoop, calls=%fused_computation.129 | loop fusion | bytes 29203456 | tf_op jit(solution)/shard_map/slice | solution.py:142
  75.3 11.6 %copy.32 = bf16[79,152,152]{1,0,2:T(8,128)(2,1)} copy(bf16[79,152,152]{0,2,1:T(8,128)(2,1)} %get-tuple-element.64) | data formatting | bytes 7300864 | tf_op jit(solution)/shard_map/slice | solution.py:142
  86.9 10.7 %reshape.132 = bf16[12008,152]{0,1:T(8,128)(2,1)} reshape(bf16[79,152,152]{1,0,2:T(8,128)(2,1)} %copy.32) | data formatting | bytes 7300864 | tf_op jit(solution)/shard_map/reshape | solution.py:142
  97.6 11.6 %copy.35 = bf16[79,152,152]{1,0,2:T(8,128)(2,1)} copy(bf16[79,152,152]{0,2,1:T(8,128)(2,1)} %get-tuple-element.63) | data formatting | bytes 7300864 | tf_op jit(solution)/shard_map/slice | solution.py:142
  109.2 10.7 %reshape.134 = bf16[12008,152]{0,1:T(8,128)(2,1)} reshape(bf16[79,152,152]{1,0,2:T(8,128)(2,1)} %copy.35) | data formatting | bytes 7300864 | tf_op jit(solution)/shard_map/reshape | solution.py:142
  119.9 11.6 %copy.38 = bf16[79,152,152]{1,0,2:T(8,128)(2,1)} copy(bf16[79,152,152]{0,2,1:T(8,128)(2,1)} %get-tuple-element.65) | data formatting | bytes 7300864 | tf_op jit(solution)/shard_map/slice | solution.py:142
  131.5 10.7 %reshape.136 = bf16[12008,152]{0,1:T(8,128)(2,1)} reshape(bf16[79,152,152]{1,0,2:T(8,128)(2,1)} %copy.38) | data formatting | bytes 7300864 | tf_op jit(solution)/shard_map/reshape | solution.py:142
  142.2 11.6 %copy.41 = bf16[79,152,152]{1,0,2:T(8,128)(2,1)} copy(bf16[79,152,152]{0,2,1:T(8,128)(2,1)} %get-tuple-element.62) | data formatting | bytes 7300864 | tf_op jit(solution)/shard_map/slice | solution.py:142
  153.9 10.7 %reshape.138 = bf16[12008,152]{0,1:T(8,128)(2,1)} reshape(bf16[79,152,152]{1,0,2:T(8,128)(2,1)} %copy.41) | data formatting | bytes 7300864 | tf_op jit(solution)/shard_map/reshape | solution.py:142
  177.9 15.4 %copy.31 = bf16[8,32,79,152]{3,2,1,0:T(8,128)(2,1)} copy(bf16[8,32,79,152]{2,3,0,1:T(8,128)(2,1)} %convert_bitcast_fusion.3) | data formatting | bytes 12296192 | tf_op jit(solution)/shard_map/convert_element_type | solution.py:140
  193.2 16.7 %reshape.131 = bf16[256,12008]{1,0:T(8,128)(2,1)} reshape(bf16[8,32,79,152]{3,2,1,0:T(8,128)(2,1)} %copy.31) | data formatting | bytes 12296192 | tf_op jit(solution)/shard_map/reshape | solution.py:141
  215.4 15.4 %copy.34 = bf16[8,32,79,152]{3,2,1,0:T(8,128)(2,1)} copy(bf16[8,32,79,152]{2,3,0,1:T(8,128)(2,1)} %convert_bitcast_fusion.2) | data formatting | bytes 12296192 | tf_op jit(solution)/shard_map/convert_element_type | solution.py:140
  230.8 16.8 %reshape.133 = bf16[256,12008]{1,0:T(8,128)(2,1)} reshape(bf16[8,32,79,152]{3,2,1,0:T(8,128)(2,1)} %copy.34) | data formatting | bytes 12296192 | tf_op jit(solution)/shard_map/reshape | solution.py:141
  253.0 15.4 %copy.37 = bf16[8,32,79,152]{3,2,1,0:T(8,128)(2,1)} copy(bf16[8,32,79,152]{2,3,0,1:T(8,128)(2,1)} %convert_bitcast_fusion.1) | data formatting | bytes 12296192 | tf_op jit(solution)/shard_map/convert_element_type | solution.py:140
  268.4 17.1 %reshape.135 = bf16[256,12008]{1,0:T(8,128)(2,1)} reshape(bf16[8,32,79,152]{3,2,1,0:T(8,128)(2,1)} %copy.37) | data formatting | bytes 12296192 | tf_op jit(solution)/shard_map/reshape | solution.py:141
  304.4 15.4 %copy.40 = bf16[8,32,79,152]{3,2,1,0:T(8,128)(2,1)} copy(bf16[8,32,79,152]{2,3,0,1:T(8,128)(2,1)} %convert_bitcast_fusion) | data formatting | bytes 12296192 | tf_op jit(solution)/shard_map/convert_element_type | solution.py:140
  319.8 16.8 %reshape.137 = bf16[256,12008]{1,0:T(8,128)(2,1)} reshape(bf16[8,32,79,152]{3,2,1,0:T(8,128)(2,1)} %copy.40) | data formatting | bytes 12296192 | tf_op jit(solution)/shard_map/reshape | solution.py:141
  360.8 444.9 %while.10 = (s32[]{:T(128)}, f32[16,4,32,128]{3,2,1,0:T(8,128)}, pred[16,4,27]{2,1,0:T(4,128)(4,1)S(1)}, s32[16,4,27]{2,1,0:T(4,128)}, f32[192,4480]{1,0:T(8,128)S(1)}, /*index=5*/f32[16,4,3,128]{3,1,0,2:T(4,128)S(1)}, s32[]{:T(128)}) while((s32[]{:T(128)}, f32[16,4,32,128]{3,2,1,0:T(8,128)}, pred[16,4,27]{2,1,0:T(4,128)(4,1)S(1)}, ...), condition=%wide.region_1.2_spmd, body=%wide.region_0.1_spmd.sunk | while | flops 695846208 | bytes 18517436 | solution.py:66
  378.3 10.3 %fusion.133 = f32[16,4,32,128]{3,2,1,0:T(8,128)} fusion(f32[16,4,32,128]{3,2,1,0:T(8,128)} %get-tuple-element.139, s32[]{:T(128)} %get-tuple-element.138, f32[4,27,32,128]{3,2,1,0:T(8,128)} %reshape.183, f32[4,128]{1,0:T(4,128)S(1)} %get-tuple-element.125, f32[4,27,128]{2,1,0:T(8,128)S(1)} %copy.99, f32[4,128]{1,0:T(4,128)S(1)} %get-tuple-element.127, ...), kind=kOutput, calls=%fused_computation.7.clone.1 | convolution fusion | flops 695402496 | bytes 2007552 | tf_op jit(solution)/shard_map/while/body/eval_jaxpr/vmap(sqp,spt->sqt)/dot_general | solution.py:52
  489.6 10.3 %fusion.133 = f32[16,4,32,128]{3,2,1,0:T(8,128)} fusion(f32[16,4,32,128]{3,2,1,0:T(8,128)} %get-tuple-element.139, s32[]{:T(128)} %get-tuple-element.138, f32[4,27,32,128]{3,2,1,0:T(8,128)} %reshape.183, f32[4,128]{1,0:T(4,128)S(1)} %get-tuple-element.125, f32[4,27,128]{2,1,0:T(8,128)S(1)} %copy.99, f32[4,128]{1,0:T(4,128)S(1)} %get-tuple-element.127, ...), kind=kOutput, calls=%fused_computation.7.clone.1 | convolution fusion | flops 695402496 | bytes 2007552 | tf_op jit(solution)/shard_map/while/body/eval_jaxpr/vmap(sqp,spt->sqt)/dot_general | solution.py:52
  517.4 10.3 %fusion.133 = f32[16,4,32,128]{3,2,1,0:T(8,128)} fusion(f32[16,4,32,128]{3,2,1,0:T(8,128)} %get-tuple-element.139, s32[]{:T(128)} %get-tuple-element.138, f32[4,27,32,128]{3,2,1,0:T(8,128)} %reshape.183, f32[4,128]{1,0:T(4,128)S(1)} %get-tuple-element.125, f32[4,27,128]{2,1,0:T(8,128)S(1)} %copy.99, f32[4,128]{1,0:T(4,128)S(1)} %get-tuple-element.127, ...), kind=kOutput, calls=%fused_computation.7.clone.1 | convolution fusion | flops 695402496 | bytes 2007552 | tf_op jit(solution)/shard_map/while/body/eval_jaxpr/vmap(sqp,spt->sqt)/dot_general | solution.py:52
  628.6 10.3 %fusion.133 = f32[16,4,32,128]{3,2,1,0:T(8,128)} fusion(f32[16,4,32,128]{3,2,1,0:T(8,128)} %get-tuple-element.139, s32[]{:T(128)} %get-tuple-element.138, f32[4,27,32,128]{3,2,1,0:T(8,128)} %reshape.183, f32[4,128]{1,0:T(4,128)S(1)} %get-tuple-element.125, f32[4,27,128]{2,1,0:T(8,128)S(1)} %copy.99, f32[4,128]{1,0:T(4,128)S(1)} %get-tuple-element.127, ...), kind=kOutput, calls=%fused_computation.7.clone.1 | convolution fusion | flops 695402496 | bytes 2007552 | tf_op jit(solution)/shard_map/while/body/eval_jaxpr/vmap(sqp,spt->sqt)/dot_general | solution.py:52
  712.0 10.3 %fusion.133 = f32[16,4,32,128]{3,2,1,0:T(8,128)} fusion(f32[16,4,32,128]{3,2,1,0:T(8,128)} %get-tuple-element.139, s32[]{:T(128)} %get-tuple-element.138, f32[4,27,32,128]{3,2,1,0:T(8,128)} %reshape.183, f32[4,128]{1,0:T(4,128)S(1)} %get-tuple-element.125, f32[4,27,128]{2,1,0:T(8,128)S(1)} %copy.99, f32[4,128]{1,0:T(4,128)S(1)} %get-tuple-element.127, ...), kind=kOutput, calls=%fused_computation.7.clone.1 | convolution fusion | flops 695402496 | bytes 2007552 | tf_op jit(solution)/shard_map/while/body/eval_jaxpr/vmap(sqp,spt->sqt)/dot_general | solution.py:52
  (398 shorter events, 507.8 us)
Async XLA Ops:
  0.0 352.8 %copy-start = (f32[8,152,152]{2,1,0:T(8,128)S(1)}, f32[8,152,152]{2,1,0:T(8,128)}, u32[]{:S(2)}) copy-start(f32[8,152,152]{2,1,0:T(8,128)} %param.23) | copy-start | bytes 2217988
  1.0 17.8 %copy-start.11 = (f32[64,152]{1,0:T(8,128)}, f32[64,152]{1,0:T(8,128)S(1)}, u32[]{:S(2)}) copy-start(f32[64,152]{1,0:T(8,128)S(1)} %get-tuple-element.66) | copy-start | bytes 116740
  1.0 17.8 %copy-start.12 = (f32[64,152]{1,0:T(8,128)}, f32[64,152]{1,0:T(8,128)S(1)}, u32[]{:S(2)}) copy-start(f32[64,152]{1,0:T(8,128)S(1)} %get-tuple-element.67) | copy-start | bytes 116740
  1.0 17.8 %copy-start.13 = (f32[64,152]{1,0:T(8,128)}, f32[64,152]{1,0:T(8,128)S(1)}, u32[]{:S(2)}) copy-start(f32[64,152]{1,0:T(8,128)S(1)} %get-tuple-element.68) | copy-start | bytes 116740
  1.9 17.0 %copy-start.15 = (f32[64,128]{1,0:T(8,128)}, f32[64,128]{1,0:T(8,128)S(1)}, u32[]{:S(2)}) copy-start(f32[64,128]{1,0:T(8,128)S(1)} %get-tuple-element.69) | copy-start | bytes 98308
  1.9 17.0 %copy-start.16 = (f32[64,128]{1,0:T(8,128)}, f32[64,128]{1,0:T(8,128)S(1)}, u32[]{:S(2)}) copy-start(f32[64,128]{1,0:T(8,128)S(1)} %get-tuple-element.70) | copy-start | bytes 98308
  1.9 17.0 %copy-start.17 = (f32[64,128]{1,0:T(8,128)}, f32[64,128]{1,0:T(8,128)S(1)}, u32[]{:S(2)}) copy-start(f32[64,128]{1,0:T(8,128)S(1)} %get-tuple-element.71) | copy-start | bytes 98308
  4.1 14.8 %copy-start.7 = (f32[152,152]{1,0:T(8,128)S(1)}, f32[152,152]{1,0:T(8,128)}, u32[]{:S(2)}) copy-start(f32[152,152]{1,0:T(8,128)} %param.20) | copy-start | bytes 277252
  23.1 147.6 %collective-permute-start = (bf16[8,4864]{1,0:T(8,128)(2,1)S(1)}, bf16[8,4864]{1,0:T(8,128)(2,1)S(1)}, u32[]{:S(2)}, u32[]{:S(2)}) collective-permute-start(bf16[8,4864]{1,0:T(8,128)(2,1)S(1)} %reshape.130), channel_id=1, source_target_pairs={{0,1},{1,2},{2,3},{3,4},{4,5},{5,6},{6,7},{7,8},{8,9},{9,10},{10,1... | collective-permute-start | bytes 233480 | tf_op jit(solution)/shard_map/ppermute | solution.py:16
  25.0 146.0 %collective-permute-start.1 = (bf16[8,4864]{1,0:T(8,128)(2,1)S(1)}, bf16[8,4864]{1,0:T(8,128)(2,1)}, u32[]{:S(2)}, u32[]{:S(2)}) collective-permute-start(bf16[8,4864]{1,0:T(8,128)(2,1)S(1)} %reshape.130), channel_id=1, source_target_pairs={{1,0},{2,1},{3,2},{4,3},{5,4},{6,5},{7,6},{8,7},{9,8},{10,9},{11,1... | collective-permute-start | bytes 233480 | tf_op jit(solution)/shard_map/ppermute | solution.py:17
  32.1 326.4 %collective-permute-start.10 = (f32[64,4480]{1,0:T(8,128)}, f32[64,4480]{1,0:T(8,128)}, u32[]{:S(2)}, u32[]{:S(2)}) collective-permute-start(f32[64,4480]{1,0:T(8,128)} %bitcast_dynamic-update-slice_fusion), channel_id=1, source_target_pairs={{1,0},{2,1},{3,2},{4,3},{5,4},{6,5},{7,6},{8,7},{9,8},{10,9},{11,1... | collective-permute-start | bytes 3440648 | tf_op jit(solution)/shard_map/ppermute | solution.py:17
  34.1 324.5 %collective-permute-start.9 = (f32[64,4480]{1,0:T(8,128)}, f32[64,4480]{1,0:T(8,128)}, u32[]{:S(2)}, u32[]{:S(2)}) collective-permute-start(f32[64,4480]{1,0:T(8,128)} %bitcast_dynamic-update-slice_fusion), channel_id=1, source_target_pairs={{0,1},{1,2},{2,3},{3,4},{4,5},{5,6},{6,7},{7,8},{8,9},{9,10},{10,1... | collective-permute-start | bytes 3440648 | tf_op jit(solution)/shard_map/ppermute | solution.py:16
  37.5 25.6 %collective-permute-start.2 = (f32[32,152]{1,0:T(8,128)S(1)}, f32[32,152]{1,0:T(8,128)S(1)}, u32[]{:S(2)}, u32[]{:S(2)}) collective-permute-start(f32[32,152]{1,0:T(8,128)S(1)} %fusion.58), channel_id=1, source_target_pairs={{0,1},{1,0},{2,3},{3,2},{4,5},{5,4},{6,7},{7,6},{8,9},{9,8},{10,11... | collective-permute-start | bytes 58376 | tf_op jit(solution)/shard_map/ppermute | solution.py:25
  40.8 22.3 %copy-start.14 = (s32[8,316]{1,0:T(8,128)S(1)}, s32[8,316]{1,0:T(8,128)}, u32[]{:S(2)}) copy-start(s32[8,316]{1,0:T(8,128)} %param.19) | copy-start | bytes 30340
  40.8 22.3 %copy-start.10 = (s32[64,27]{0,1:T(8,128)S(1)}, s32[64,27]{0,1:T(8,128)}, u32[]{:S(2)}) copy-start(s32[64,27]{0,1:T(8,128)} %param.18) | copy-start | bytes 20740
  63.2 4.0 collective-permute-start.3
  67.2 5.4 collective-permute-start.4
  72.8 92.5 %collective-permute-start.5 = (f32[32,152]{1,0:T(8,128)S(1)}, f32[32,152]{1,0:T(8,128)S(1)}, u32[]{:S(2)}, u32[]{:S(2)}) collective-permute-start(f32[32,152]{1,0:T(8,128)S(1)} %fusion.55), channel_id=1, source_target_pairs={{0,8},{1,9},{2,10},{3,11},{4,12},{5,13},{6,14},{7,15},{8,0},{9,1},... | collective-permute-start | bytes 58376 | tf_op jit(solution)/shard_map/ppermute | solution.py:25
  153.8 18.5 %copy-start.20 = (pred[8,79]{1,0:T(8,128)(4,1)S(1)}, pred[8,79]{1,0:T(8,128)(4,1)}, u32[]{:S(2)}) copy-start(pred[8,79]{1,0:T(8,128)(4,1)} %get-tuple-element.79) | copy-start | bytes 1900
  165.3 171.2 %collective-permute-start.6 = (f32[32,152]{1,0:T(8,128)S(1)}, f32[32,152]{1,0:T(8,128)S(1)}, u32[]{:S(2)}, u32[]{:S(2)}) collective-permute-start(f32[32,152]{1,0:T(8,128)S(1)} %add.90), channel_id=1, source_target_pairs={{0,16},{1,17},{2,18},{3,19},{4,20},{5,21},{6,22},{7,23},{8,24},{9,... | collective-permute-start | bytes 58376 | tf_op jit(solution)/shard_map/ppermute | solution.py:25
  193.2 16.8 %copy-start.19 = (pred[8,79]{1,0:T(8,128)(4,1)S(1)}, pred[8,79]{1,0:T(8,128)(4,1)}, u32[]{:S(2)}) copy-start(pred[8,79]{1,0:T(8,128)(4,1)} %get-tuple-element.78) | copy-start | bytes 1900
  230.8 16.8 %copy-start.18 = (pred[8,79]{1,0:T(8,128)(4,1)S(1)}, pred[8,79]{1,0:T(8,128)(4,1)}, u32[]{:S(2)}) copy-start(pred[8,79]{1,0:T(8,128)(4,1)} %get-tuple-element.77) | copy-start | bytes 1900
  336.5 8.1 collective-permute-start.7
  344.9 5.7 collective-permute-start.8
  (10 other events, 76.5 us)
where the time goes:
time: 831 us; the launch traced here: 816 us
  local copies, waits for them, and re-layouts  466 us (56%)
  matrix products  245 us (29%)
  other arithmetic  66.6 us (8%)
  starting transfers between devices  24.3 us (3%)
  waiting for transfers between devices  11.9 us (1%)
    dot_general x16, matrix products, one_leaf(): jnp.einsum('sqp,spt->sqt', weights, kernels, precision=HIGHEST, preferred...  165 us
    gather x32, local copies, waits for them, and re-layouts, one_leaf(): picked = flat_sources[leaf_ids]  91.9 us
    slice x5, local copies, waits for them, and re-layouts, local(): translate[lower_type:lower_type + type_block]  68.8 us
    reshape x4, local copies, waits for them, and re-layouts, local(): picked = picked.reshape(node_count * q_width, type_block * eq_width)  67.4 us
    convert_element_type x4, local copies, waits for them, and re-layouts, local(): picked = jnp.einsum('ntm,mqe->nqte', selector, cycle_view, preferred_elem...  61.4 us
    select_n x16, other arithmetic, one_leaf(): jnp.where(leaf_usable[:, None], picked[:, coord_len:], 0.0)  51.3 us
    reshape x16, local copies, waits for them, and re-layouts, one_leaf(): jnp.where(leaf_usable[:, None], picked[:, coord_len:], 0.0)  47.3 us
    reshape x4, local copies, waits for them, and re-layouts, local(): translate[lower_type:lower_type + type_block]  42.6 us
  transfers between devices with their start and end apart: 11, of which 3 were waited for; matrix products, arithmetic and copies ran while one was open for 37% of the time, Pallas kernels for 0%

commit v1 on v0

v1 whole, which is shorter than its diff:
```python
import functools

import jax
import jax.numpy as jnp
from jax import lax
from jax.experimental import pallas as pl
from jax.experimental.pallas import tpu as pltpu
from jax.sharding import PartitionSpec as P

HIGHEST = lax.Precision.HIGHEST
BF = jnp.bfloat16
F32 = jnp.float32
LIST = 128


def split2(x):
    hi = x.astype(BF)
    lo = (x - hi.astype(F32)).astype(BF)
    return hi, lo


def split3(x):
    a = x.astype(BF).astype(F32)
    r = x - a
    b = r.astype(BF).astype(F32)
    return a, b, r - b


def rows8(shape):
    return lax.broadcasted_iota(jnp.int32, shape, 0)


LOG2E = 1.4426950408889634


def source_tiles(coords):
    out = []
    norm = None
    row = rows8((8, 128))
    for c in coords:
        x = jnp.broadcast_to(c, (8, 128))
        a, b, d = split3(LOG2E * x)
        first = (row <= 1) | (row == 4)
        out.append(jnp.where(first, a, jnp.where(row <= 3, b, jnp.where(row == 5, d, 0.0))))
        norm = x * x if norm is None else norm + x * x
    a, b, d = split3((-0.5 * LOG2E) * norm)
    out.append(
        jnp.where(row == 0, a, jnp.where(row == 1, b, jnp.where(row == 2, d, jnp.where(row <= 5, 1.0, 0.0))))
    )
    return out


def target_tiles(coords):
    out = []
    norm = None
    row = rows8((8, 128))
    for c in coords:
        x = jnp.broadcast_to(c, (8, 128))
        a, b, d = split3(x)
        first = (row == 0) | (row == 2) | (row == 5)
        second = (row == 1) | (row == 3)
        out.append(jnp.where(first, a, jnp.where(second, b, jnp.where(row == 4, d, 0.0))))
        norm = x * x if norm is None else norm + x * x
    a, b, d = split3((-0.5 * LOG2E) * norm)
    out.append(
        jnp.where(row <= 2, 1.0, jnp.where(row == 3, a, jnp.where(row == 4, b, jnp.where(row == 5, d, 0.0))))
    )
    return out


def near_kernel(leaves, cnt, units, ptr, leaf, total_ref, p0, p1, p2, d0, d1, d2, surf, down, out, f_s, m_s, w_s, e_s, acc):
    lane = lax.broadcasted_iota(jnp.int32, (32, 128), 1)
    lane_big = lax.broadcasted_iota(jnp.int32, (128, 128), 1)
    zero_unit = 4 * (3 * leaves + 2 * leaves)

    def put_features(coords4, base_units):
        tiles = []
        for coords in coords4:
            tiles += source_tiles(coords)
        turned = jnp.concatenate(tiles, axis=0).astype(BF).T
        for i in range(4):
            own = (lane_big >= 32 * i) & (lane_big < 32 * i + 32)
            f_s[pl.ds(base_units[i], 4)] = jnp.where(own, turned, jnp.zeros_like(turned)).reshape(4, 32, 128)

    def put_density(tile, base):
        for k in range(4):
            r = tile if k == 0 else pltpu.roll(tile, 32 * k, 1)
            hi, lo = split2(r)
            m_s[base + k] = jnp.concatenate([hi, lo], axis=0)

    for slab, (p, d) in enumerate(((p0, d0), (p1, d1), (p2, d2))):

        def prep(g, carry, slab=slab, p=p, d=d):
            coords4 = [[p[c, pl.ds(4 * g + i, 1), :] for c in range(3)] for i in range(4)]
            put_features(coords4, [4 * (slab * leaves + 4 * g + i) for i in range(4)])
            for i in range(4):
                j = 4 * g + i
                masked = jnp.where(lane < cnt[slab * leaves + j], d[j], 0.0)
                put_density(masked, 4 * (slab * leaves + j))
            return carry

        lax.fori_loop(0, leaves // 4, prep, 0)

    def prep_surface(g, carry):
        coords4 = [[surf[3 * (i % 2) + c, pl.ds(2 * g + i // 2, 1), :] for c in range(3)] for i in range(4)]
        put_features(coords4, [4 * (3 * leaves + 4 * g + i) for i in range(4)])
        for i in range(4):
            put_density(down[2 * g + i // 2, :, pl.ds(128 * (i % 2), 128)], 4 * (3 * leaves + 4 * g + i))
        return carry

    lax.fori_loop(0, leaves // 2, prep_surface, 0)
    f_s[pl.ds(zero_unit, 4)] = jnp.zeros((4, 32, 128), BF)
    m_s[pl.ds(zero_unit, 4)] = jnp.zeros((4, 64, 128), BF)

    def prep_target(j, carry):
        tile = jnp.concatenate(target_tiles([p1[c, pl.ds(j, 1), :] for c in range(3)]), axis=0).astype(BF)
        w_s[j] = jnp.concatenate([tile] * 4, axis=0)
        acc[j] = jnp.zeros((64, 256), F32)
        return carry

    lax.fori_loop(0, leaves, prep_target, 0)

    lane64 = lax.broadcasted_iota(jnp.int32, (64, 128), 1)

    def exponents(i, slot):
        base, l = ptr[i], leaf[i]
        left = jnp.concatenate([f_s[units[base + v]] for v in range(4)], axis=0)
        right = jnp.concatenate([f_s[units[base + 4 + v]] for v in range(4)], axis=0)
        w = w_s[l]
        e_s[slot, 0] = jnp.dot(left, w, preferred_element_type=F32)
        e_s[slot, 1] = jnp.dot(right, w, preferred_element_type=F32)

    def weights(base):
        t = [m_s[units[base + v]] for v in range(4)]
        return jnp.where(
            lane64 < 64, jnp.where(lane64 < 32, t[0], t[1]), jnp.where(lane64 < 96, t[2], t[3])
        )

    def apply(i, slot):
        base, l = ptr[i], leaf[i]
        m = jnp.concatenate([weights(base + 8), weights(base + 12)], axis=1)
        k = jnp.exp2(e_s[slot].reshape(256, 128))
        hi, lo = split2(k)
        acc[l] += jnp.dot(m, jnp.concatenate([hi, lo], axis=1), preferred_element_type=F32)

    half = 4
    for u in range(half):
        exponents(u, u)

    def body(i, carry):
        at = 2 * half * i
        for u in range(half):
            exponents(at + half + u, half + u)
            apply(at + u, u)
        for u in range(half):
            exponents(at + 2 * half + u, u)
            apply(at + half + u, half + u)
        return carry

    lax.fori_loop(0, total_ref[0], body, 0)

    def finish(j, carry):
        a = acc[j]
        v = (a[:32, :128] + a[:32, 128:]) + (a[32:, :128] + a[32:, 128:])
        out[j] = jnp.where(lane < cnt[leaves + j], v, 0.0)
        return carry

    lax.fori_loop(0, leaves, finish, 0)


def near_call(cnt, units_list, ptr, leaf, total, pts, dens, surf, down):
    leaves = dens[0].shape[0]
    units = 4 * (3 * leaves + 2 * leaves) + 4
    smem = pl.BlockSpec(memory_space=pltpu.SMEM)
    vmem = pl.BlockSpec(memory_space=pltpu.VMEM)
    return pl.pallas_call(
        functools.partial(near_kernel, leaves),
        out_shape=jax.ShapeDtypeStruct(dens[0].shape, F32),
        in_specs=[smem] * 5 + [vmem] * 8,
        out_specs=vmem,
        scratch_shapes=[
            pltpu.VMEM((units, 32, 128), BF),
            pltpu.VMEM((units, 64, 128), BF),
            pltpu.VMEM((leaves, 128, 128), BF),
            pltpu.VMEM((8, 2, 128, 128), F32),
            pltpu.VMEM((leaves, 64, 256), F32),
        ],
        compiler_params=pltpu.CompilerParams(vmem_limit_bytes=60 * 1024 * 1024),
        name="near",
    )(cnt, units_list, ptr, leaf, total, *pts, *dens, surf, down)


def make_lists(ulist, counts3, first):
    leaves = ulist.shape[0]
    ids = jnp.arange(3 * leaves)
    rel = jnp.where(ulist >= 0, ulist - first, -1)
    cnt = jnp.sum(jnp.where(rel[:, :, None] == ids, counts3, 0), axis=-1)
    num = (cnt + 31) // 32
    slots = ulist.shape[1]
    before = jnp.arange(slots)[:, None] < jnp.arange(slots)[None, :]
    start = 5 + jnp.sum(jnp.where(before, num[:, :, None], 0), axis=1)
    place = jnp.arange(LIST)
    at = place - start[:, :, None]
    inside = (at >= 0) & (at < num[:, :, None])
    zero_unit = 20 * leaves
    unit = zero_unit + jnp.sum(jnp.where(inside, 4 * rel[:, :, None] + at - zero_unit, 0), axis=1)
    surface_unit = 12 * leaves + 8 * jnp.arange(leaves)[:, None] + place
    unit = jnp.where(place < 5, surface_unit, unit).astype(jnp.int32)
    turned = (unit - unit % 4) + (place - unit) % 4
    n = (5 + jnp.sum(num, axis=1) + 7) // 8
    upto = jnp.arange(leaves)[:, None] <= jnp.arange(leaves)[None, :]
    end = jnp.sum(jnp.where(upto, n[:, None], 0), axis=0)
    begin = end - n
    chunk = jnp.arange(16 * leaves + 16)
    inside = (chunk[:, None] >= begin) & (chunk[:, None] < end)
    leaf = jnp.sum(jnp.where(inside, jnp.arange(leaves), 0), axis=1)
    ptr = jnp.sum(jnp.where(inside, 16 * (16 * jnp.arange(leaves) + chunk[:, None] - begin), 0), axis=1)
    ptr = jnp.where(chunk < end[-1], ptr, 256 * leaves)
    both = jnp.stack([unit.reshape(leaves, 16, 8), turned.reshape(leaves, 16, 8)], axis=2).reshape(-1)
    both = jnp.concatenate([both, jnp.full((16,), zero_unit)])
    rounds = ((end[-1] + 7) // 8).reshape(1)
    return [v.astype(jnp.int32) for v in (both, ptr, leaf, rounds)]


def far_kernel(step, table, sel, nodes, out):
    width = table.shape[1]
    lane = lax.broadcasted_iota(jnp.int32, (32, 128), 1)

    @pl.when(pl.program_id(0) == 0)
    def _():
        out[...] = jnp.zeros_like(out)

    zero = jnp.zeros((32, 128), BF)
    picks = sel[...]
    total = None
    for k in range(0, step, 2):
        sums = []
        for e in (k, k + 1):
            s = jnp.dot(table[e], picks, preferred_element_type=F32)
            hi, lo = split2(s)
            sums.append(jnp.concatenate([hi, lo], axis=0))
        rows = []
        for e in (k, k + 1):
            x = nodes[e]
            for n in range(8):
                own = (lane >= 32 * (n % 4)) & (lane < 32 * (n % 4) + 32)
                part = jnp.where(own, x, zero)
                rows.append(jnp.concatenate([part, zero] if n < 4 else [zero, part], axis=1))
        r = jnp.dot(
            jnp.concatenate(sums, axis=1), jnp.concatenate(rows, axis=0), preferred_element_type=F32
        )
        r = r[:width] + r[width:]
        total = r if total is None else total + r
    out[...] += total


def far_call(table, sel, nodes):
    count, width, types = table.shape
    step = 8
    return pl.pallas_call(
        lambda *refs: far_kernel(step, *refs),
        grid=(count // step,),
        out_shape=jax.ShapeDtypeStruct((width, 256), F32),
        in_specs=[
            pl.BlockSpec((step, width, types), lambda i: (i, 0, 0)),
            pl.BlockSpec((types, 256), lambda i: (0, 0)),
            pl.BlockSpec((step, 32, 128), lambda i: (i, 0, 0)),
        ],
        out_specs=pl.BlockSpec((width, 256), lambda i: (0, 0)),
        compiler_params=pltpu.CompilerParams(vmem_limit_bytes=48 * 1024 * 1024),
        name="far",
    )(table, sel, nodes)


def far_inputs(vlist, base, cycle):
    rel = jnp.where(vlist >= 0, vlist - base, -1)
    sel = (rel.T[:, :, None] == jnp.arange(32)).astype(BF).reshape(rel.shape[1], 256)
    turned = jnp.transpose(cycle, (2, 0, 1))
    nodes = jnp.pad(jnp.concatenate([turned] * 4, axis=2), ((0, 0), (0, 8), (0, 0)))
    return sel, nodes


def extended(value, sides, width):
    for axis, dim in sides:
        count, length = (lax.axis_size(axis), value.shape[dim])
        up = [(i, (i + 1) % count) for i in range(count - 1)]
        down = [(j, i) for i, j in up]
        last = lax.slice_in_dim(value, length - width, length, axis=dim)
        first = lax.slice_in_dim(value, 0, width, axis=dim)
        before = lax.ppermute(last, axis, up)
        after = lax.ppermute(first, axis, down)
        value = jnp.concatenate([before, value, after], axis=dim)
    return value


def swapped(value, axis, bit):
    mask = 2**bit
    pairs = [(source, source ^ mask) for source in range(lax.axis_size(axis))]
    return lax.ppermute(value, axis, pairs)


def kernel(left_pts, right_pts):
    total_sq = jnp.zeros((left_pts.shape[1], right_pts.shape[1]), jnp.float32)
    for coord_index in range(3):
        offset = left_pts[coord_index][:, None] - right_pts[coord_index][None, :]
        total_sq = total_sq + offset * offset
    return jnp.exp(-0.5 * total_sq)


def local(
    points,
    dens,
    surface,
    counts,
    ulist,
    vlist,
    up_inverse,
    down_inverse,
    shift_up,
    shift_down,
    coarse,
    translate,
):
    leaf_count, q_width, p_width = dens.shape
    eq_width = surface.shape[2]
    node_count = vlist.shape[0]
    index = lax.axis_index("oct")
    slots = jnp.arange(p_width)
    mask = (slots[None, :] < counts[:, None]).astype(jnp.float32)[:, None, :]
    masked = dens * mask
    count = lax.axis_size("oct")
    up = [(i, (i + 1) % count) for i in range(count - 1)]
    down = [(i, j) for j, i in up]
    turned_points = jnp.transpose(points, (1, 0, 2))
    points3 = [lax.ppermute(turned_points, "oct", up), turned_points, lax.ppermute(turned_points, "oct", down)]
    dens3 = [lax.ppermute(dens, "oct", up), dens, lax.ppermute(dens, "oct", down)]
    counts3 = jnp.concatenate([lax.ppermute(counts, "oct", up), counts, lax.ppermute(counts, "oct", down)])
    lists = make_lists(ulist, counts3, (index - 1) * leaf_count)
    up_kernel = jax.vmap(kernel)(points, surface)
    check = jnp.einsum("lqp,lpe->lqe", masked, up_kernel, precision=HIGHEST)
    leaf_eq = jnp.dot(
        check.reshape(-1, eq_width),
        up_inverse,
        precision=HIGHEST,
        preferred_element_type=jnp.float32,
    ).reshape(leaf_count, q_width, eq_width)
    node_eq = jnp.einsum(
        "ncqe,cef->nqf", leaf_eq.reshape(-1, 8, q_width, eq_width), shift_up, precision=HIGHEST
    )
    node_send = node_eq.astype(jnp.bfloat16).reshape(node_count, q_width * eq_width)
    slab_eq = jnp.einsum("cqe,cef->qf", node_eq, shift_up, precision=HIGHEST)
    cycle = extended(node_send, (("oct", 0),), node_count)
    bit_count = lax.axis_size("oct").bit_length() - 1
    slab_local = jnp.zeros((q_width, eq_width), jnp.float32)
    current = slab_eq
    for level_start in range(0, bit_count, 3):
        width_bits = min(3, bit_count - level_start)
        child_slot = jnp.right_shift(index, level_start) & 7
        current = jnp.dot(
            current, shift_up[child_slot], precision=HIGHEST, preferred_element_type=jnp.float32
        )
        for bit_number in range(level_start, level_start + width_bits):
            current = current + swapped(current, "oct", bit_number)
        slab_local = slab_local + jnp.dot(
            current, coarse[child_slot], precision=HIGHEST, preferred_element_type=jnp.float32
        )
    cycle = cycle.reshape(3 * node_count, q_width, eq_width)
    sel, nodes = far_inputs(vlist, (index - 1) * node_count, cycle)
    far_node = far_call(jnp.transpose(translate, (1, 2, 0)), sel, nodes)
    far_node = far_node.T.reshape(node_count, q_width, eq_width)
    parent_part = jnp.einsum("qe,cef->cqf", slab_local, shift_down, precision=HIGHEST)
    node_local = far_node + parent_part
    leaf_local = jnp.einsum("nqe,cef->ncqf", node_local, shift_down, precision=HIGHEST).reshape(
        leaf_count, q_width, eq_width
    )
    wide = 256
    pad = wide - eq_width
    leaf_down = jnp.dot(
        leaf_local.reshape(-1, eq_width),
        jnp.pad(down_inverse, ((0, 0), (0, pad))),
        precision=HIGHEST,
        preferred_element_type=jnp.float32,
    ).reshape(leaf_count, q_width, wide)
    surf = jnp.pad(jnp.transpose(surface, (1, 0, 2)), ((0, 0), (0, 0), (0, pad)))
    surf = jnp.concatenate([surf[:, :, :128], surf[:, :, 128:]], axis=0)
    return near_call(counts3, *lists, points3, dens3, surf, leaf_down)


def solution(mesh):
    placed = (
        P("oct", None, None),
        P("oct", None, None),
        P("oct", None, None),
        P("oct"),
        P("oct", None),
        P("oct", None),
        P(),
        P(),
        P(),
        P(),
        P(),
        P(),
    )
    return jax.shard_map(
        local, mesh=mesh, in_specs=placed, out_specs=P("oct", None, None), check_vma=False
    )
```

time: 831 us -> 188 us (0.23)
  the two profiles are of different devices: /device:TPU:6 before, /device:TPU:31 now
where the time goes in v1:
time: 188 us; the launch traced here: 187 us
  Pallas kernels  69.5 us (37%)
  starting transfers between devices  47.5 us (25%)
  matrix products  29.7 us (16%)
  other arithmetic  14.6 us (8%)
  local copies, waits for them, and re-layouts  12.3 us (7%)
  waiting for transfers between devices  12 us (6%)
    pallas_call x1, Pallas kernels, near_call(): pl.pallas_call(functools.partial(near_kernel, leaves), out_shape=jax.Shap...  47.7 us
    pallas_call x1, Pallas kernels, far_call(): pl.pallas_call(lambda *refs: far_kernel(step, *refs), grid=(count // step...  21.8 us
    dot_general x1, matrix products, local(): check = jnp.einsum('lqp,lpe->lqe', masked, up_kernel, precision=HIGHEST)  14 us
    ppermute x7, waiting for transfers between devices, swapped(): return lax.ppermute(value, axis, pairs)  12 us
    ppermute x7, starting transfers between devices, swapped(): return lax.ppermute(value, axis, pairs)  10.2 us
    ppermute x1, starting transfers between devices, local(): lax.ppermute(dens, 'oct', up)  10.2 us
    ppermute x1, starting transfers between devices, local(): lax.ppermute(turned_points, 'oct', up)  7.86 us
    ppermute x1, starting transfers between devices, local(): lax.ppermute(counts, 'oct', up)  7.86 us
  transfers between devices with their start and end apart: 15, of which 4 were waited for; matrix products, arithmetic and copies ran while one was open for 19% of the time, Pallas kernels for 12%

profile of v1, /device:TPU:31, one launch (start us, length us, event | category | flops | bytes accessed | tf_op | source)
XLA Modules:
  0.0 186.8 jit_solution(829595416676207301)
XLA Ops:
  2.6 14.0 %fusion = f32[64,32,152]{2,1,0:T(8,128)S(1)} fusion(f32[64,152]{1,0:T(8,128)S(1)} %get-tuple-element.14, f32[64,128]{1,0:T(8,128)S(1)} %get-tuple-element.19, f32[64,152]{1,0:T(8,128)S(1)} %get-tuple-element.15, f32[64,128]{1,0:T(8,128)S(1)} %get-tuple-element.20, f32[64,152]{1,0:T(8,128)S(1)} %get-tuple-element.13, f32[64,128]{1,0:T(8,128)S(1)} %get-tuple-element.18, ...), kind=kOutput, calls=%fused_computation | convolution fusion | flops 489619456 | bytes 2541568 | tf_op jit(solution)/shard_map/lqp,lpe->lqe/dot_general | solution.py:340
  16.6 1.9 %fusion.42 = f32[8,8,32,152]{3,2,1,0:T(8,128)S(1)} fusion(f32[8,8,32,152]{3,2,1,0:T(8,128)S(1)} %bitcast.96, f32[152,152]{1,0:T(8,128)S(1)} %copy-done.3), kind=kOutput, calls=%fused_computation.57 | convolution fusion | flops 567803904 | bytes 2582784 | tf_op jit(solution)/shard_map/dot_general | solution.py:341
  18.5 2.0 %fusion.89 = (bf16[8,32,152]{2,1,0:T(8,128)(2,1)S(1)}, f32[8,32,152]{2,1,0:T(8,128)S(1)}) fusion(f32[8,8,32,152]{3,2,1,0:T(8,128)S(1)} %fusion.42, f32[8,152,152]{2,1,0:T(8,128)S(1)} %copy-done.1), kind=kOutput, calls=%fused_computation.142 | convolution fusion | flops 567842816 | bytes 2217984 | tf_op jit(solution)/shard_map/ncqe,cef->nqf/dot_general | solution.py:347
  21.4 3.7 %collective-permute-start.6 = (bf16[8,4864]{1,0:T(8,128)(2,1)}, bf16[8,4864]{1,0:T(8,128)(2,1)}, u32[]{:S(2)}, u32[]{:S(2)}) collective-permute-start(bf16[8,4864]{1,0:T(8,128)(2,1)} %reshape.266), channel_id=1, source_target_pairs={{0,1},{1,2},{2,3},{3,4},{4,5},{5,6},{6,7},{7,8},{8,9},{9,10},{10,1... | collective-permute-start | bytes 233480 | tf_op jit(solution)/shard_map/ppermute | solution.py:290
  25.1 1.9 %collective-permute-start.7 = (bf16[8,4864]{1,0:T(8,128)(2,1)}, bf16[8,4864]{1,0:T(8,128)(2,1)}, u32[]{:S(2)}, u32[]{:S(2)}) collective-permute-start(bf16[8,4864]{1,0:T(8,128)(2,1)} %reshape.266), channel_id=1, source_target_pairs={{1,0},{2,1},{3,2},{4,3},{5,4},{6,5},{7,6},{8,7},{9,8},{10,9},{11,1... | collective-permute-start | bytes 233480 | tf_op jit(solution)/shard_map/ppermute | solution.py:291
  27.0 7.9 %collective-permute-start = (s32[64]{0:T(128)S(1)}, s32[64]{0:T(128)}, u32[]{:S(2)}, u32[]{:S(2)}) collective-permute-start(s32[64]{0:T(128)S(1)} %copy-done.7), channel_id=1, source_target_pairs={{0,1},{1,2},{2,3},{3,4},{4,5},{5,6},{6,7},{7,8},{8,9},{9,10},{10,1... | collective-permute-start | bytes 776 | tf_op jit(solution)/shard_map/ppermute | solution.py:337
  34.9 1.9 %collective-permute-start.1 = (s32[64]{0:T(128)S(1)}, s32[64]{0:T(128)}, u32[]{:S(2)}, u32[]{:S(2)}) collective-permute-start(s32[64]{0:T(128)S(1)} %copy-done.7), channel_id=1, source_target_pairs={{1,0},{2,1},{3,2},{4,3},{5,4},{6,5},{7,6},{8,7},{9,8},{10,9},{11,1... | collective-permute-start | bytes 776 | tf_op jit(solution)/shard_map/ppermute | solution.py:337
  36.8 7.9 %collective-permute-start.2 = (f32[3,64,128]{2,1,0:T(8,128)}, f32[3,64,128]{2,1,0:T(8,128)}, u32[]{:S(2)}, u32[]{:S(2)}) collective-permute-start(f32[3,64,128]{2,1,0:T(8,128)} %bitcast.3.p1), channel_id=1, source_target_pairs={{0,1},{1,2},{2,3},{3,4},{4,5},{5,6},{6,7},{7,8},{8,9},{9,10},{10,1... | collective-permute-start | bytes 294920 | tf_op jit(solution)/shard_map/ppermute | solution.py:335
  46.4 1.4 convolution_bitcast_fusion.1
  50.6 1.9 %collective-permute-start.3 = (f32[3,64,128]{2,1,0:T(8,128)}, f32[3,64,128]{2,1,0:T(8,128)}, u32[]{:S(2)}, u32[]{:S(2)}) collective-permute-start(f32[3,64,128]{2,1,0:T(8,128)} %bitcast.3.p1), channel_id=1, source_target_pairs={{1,0},{2,1},{3,2},{4,3},{5,4},{6,5},{7,6},{8,7},{9,8},{10,9},{11,1... | collective-permute-start | bytes 294920 | tf_op jit(solution)/shard_map/ppermute | solution.py:335
  56.6 1.5 select_reduce_fusion.3
  60.6 3.0 %collective-permute-done.10 = f32[32,152]{1,0:T(8,128)S(1)} collective-permute-done((f32[32,152]{1,0:T(8,128)S(1)}, f32[32,152]{1,0:T(8,128)S(1)}, u32[]{:S(2)}, u32[]{:S(2)}) %collective-permute-start.10) | collective-permute-done | bytes 19488 | tf_op jit(solution)/shard_map/ppermute | solution.py:299
  65.9 2.7 %reshape.264 = s32[16384]{0:T(1024)S(1)} reshape(s32[64,16,2,8]{3,2,1,0:T(2,128)} %copy.43) | data formatting | bytes 131072 | tf_op jit(solution)/shard_map/reshape | solution.py:219
  69.3 10.2 %collective-permute-start.4 = (f32[64,32,128]{2,1,0:T(8,128)}, f32[64,32,128]{2,1,0:T(8,128)}, u32[]{:S(2)}, u32[]{:S(2)}) collective-permute-start(f32[64,32,128]{2,1,0:T(8,128)} %d1.1), channel_id=1, source_target_pairs={{0,1},{1,2},{2,3},{3,4},{4,5},{5,6},{6,7},{7,8},{8,9},{9,10},{10,1... | collective-permute-start | bytes 3145736 | tf_op jit(solution)/shard_map/ppermute | solution.py:336
  79.4 1.9 %collective-permute-start.5 = (f32[64,32,128]{2,1,0:T(8,128)}, f32[64,32,128]{2,1,0:T(8,128)}, u32[]{:S(2)}, u32[]{:S(2)}) collective-permute-start(f32[64,32,128]{2,1,0:T(8,128)} %d1.1), channel_id=1, source_target_pairs={{1,0},{2,1},{3,2},{4,3},{5,4},{6,5},{7,6},{8,7},{9,8},{10,9},{11,1... | collective-permute-start | bytes 3145736 | tf_op jit(solution)/shard_map/ppermute | solution.py:336
  85.6 6.6 %collective-permute-done.12 = f32[32,152]{1,0:T(8,128)} collective-permute-done((f32[32,152]{1,0:T(8,128)S(1)}, f32[32,152]{1,0:T(8,128)}, u32[]{:S(2)}, u32[]{:S(2)}) %collective-permute-start.12) | collective-permute-done | bytes 19488 | tf_op jit(solution)/shard_map/ppermute | solution.py:299
  93.0 8.2 %collective-permute-start.13 = (f32[32,152]{1,0:T(8,128)S(1)}, f32[32,152]{1,0:T(8,128)S(1)}, u32[]{:S(2)}, u32[]{:S(2)}) collective-permute-start(f32[32,152]{1,0:T(8,128)S(1)} %add.264), channel_id=1, source_target_pairs={{0,32},{1,33},{2,34},{3,35},{4,36},{5,37},{6,38},{7,39},{8,40},{9,... | collective-permute-start | bytes 58376 | tf_op jit(solution)/shard_map/ppermute | solution.py:299
  101.2 3.4 %fusion.24.refs_2_ = bf16[152,32,128]{2,1,0:T(8,128)(2,1)S(1)} fusion(bf16[152,24,32]{2,1,0:T(8,128)(2,1)} %bitcast.95), kind=kLoop, calls=%fused_computation.27 | loop fusion | flops 8093696 | bytes 1478656 | tf_op jit(solution)/shard_map/concatenate | solution.py:279
  104.6 21.8 %far.1 = f32[152,256]{1,0:T(8,128)S(1)} custom-call(bf16[152,152,316]{2,1,0:T(8,128)(2,1)} %bitcast.93, bf16[316,256]{1,0:T(8,128)(2,1)S(1)} %compare_convert_fusion.refs_1_, bf16[152,32,128]{2,1,0:T(8,128)(2,1)S(1)} %fusion.24.refs_2_), custom_call_target="tpu_custom_call" | custom-call | tf_op jit(solution)/shard_map/far/pallas_call | solution.py:260
  126.7 1.5 collective-permute-start.14
  129.3 1.7 collective-permute-done.14
  134.0 1.8 fusion.25
  135.9 3.1 %fusion.44.down = f32[64,32,256]{2,1,0:T(8,128)} fusion(f32[64,32,152]{2,1,0:T(8,128)S(1)} %bitcast.94, f32[152,152]{1,0:T(8,128)S(1)} %copy-done.4), kind=kOutput, calls=%fused_computation.59 | convolution fusion | flops 956301312 | bytes 3434752 | tf_op jit(solution)/shard_map/dot_general | solution.py:378
  139.0 47.7 %near.1 = f32[64,32,128]{2,1,0:T(8,128)} custom-call(s32[192]{0:T(256)} %copy-done.6, s32[16400]{0:T(1024)} %concatenate.21.units, s32[1040]{0:T(1024)} %fusion.78.ptr, s32[1040]{0:T(1024)} %get-tuple-element.5.leaf, s32[1]{0:T(128)} %bitcast.2.total_ref, f32[3,64,128]{2,1,0:T(8,128)} %collective-permute-done.2.p0, f32[3,64,128]{2,1,0:T(8,128)} %bitcast.3.p1, ...), custom_call_target="tpu_custom_call" | custom-call | tf_op jit(solution)/shard_map/near/pallas_call | solution.py:176
  (84 shorter events, 26.1 us)
Async XLA Ops:
  0.0 133.3 %copy-start = (f32[8,152,152]{2,1,0:T(8,128)S(1)}, f32[8,152,152]{2,1,0:T(8,128)}, u32[]{:S(2)}) copy-start(f32[8,152,152]{2,1,0:T(8,128)} %param.21) | copy-start | bytes 2217988
  2.6 14.0 %copy-start.3 = (f32[152,152]{1,0:T(8,128)S(1)}, f32[152,152]{1,0:T(8,128)}, u32[]{:S(2)}) copy-start(f32[152,152]{1,0:T(8,128)} %param.18) | copy-start | bytes 277252
  16.6 1.9 %copy-start.1 = (f32[8,152,152]{2,1,0:T(8,128)S(1)}, f32[8,152,152]{2,1,0:T(8,128)}, u32[]{:S(2)}) copy-start(f32[8,152,152]{2,1,0:T(8,128)} %param.20) | copy-start | bytes 2217988
  18.5 8.5 %copy-start.7 = (s32[64]{0:T(128)S(1)}, s32[64]{0:T(128)}, u32[]{:S(2)}) copy-start(s32[64]{0:T(128)} %param.15) | copy-start | bytes 772
  18.5 29.4 %copy-start.5 = (s32[8,316]{1,0:T(8,128)S(1)}, s32[8,316]{1,0:T(8,128)}, u32[]{:S(2)}) copy-start(s32[8,316]{1,0:T(8,128)} %param.17) | copy-start | bytes 30340
  20.5 27.6 %copy-start.2 = (f32[64,3,152]{2,0,1:T(8,128)S(1)}, f32[64,3,152]{2,0,1:T(8,128)}, u32[]{:S(2)}) copy-start(f32[64,3,152]{2,0,1:T(8,128)} %param.14) | copy-start | bytes 350212
  21.4 58.0 %collective-permute-start.6 = (bf16[8,4864]{1,0:T(8,128)(2,1)}, bf16[8,4864]{1,0:T(8,128)(2,1)}, u32[]{:S(2)}, u32[]{:S(2)}) collective-permute-start(bf16[8,4864]{1,0:T(8,128)(2,1)} %reshape.266), channel_id=1, source_target_pairs={{0,1},{1,2},{2,3},{3,4},{4,5},{5,6},{6,7},{7,8},{8,9},{9,10},{10,1... | collective-permute-start | bytes 233480 | tf_op jit(solution)/shard_map/ppermute | solution.py:290
  25.1 57.6 %collective-permute-start.7 = (bf16[8,4864]{1,0:T(8,128)(2,1)}, bf16[8,4864]{1,0:T(8,128)(2,1)}, u32[]{:S(2)}, u32[]{:S(2)}) collective-permute-start(bf16[8,4864]{1,0:T(8,128)(2,1)} %reshape.266), channel_id=1, source_target_pairs={{1,0},{2,1},{3,2},{4,3},{5,4},{6,5},{7,6},{8,7},{9,8},{10,9},{11,1... | collective-permute-start | bytes 233480 | tf_op jit(solution)/shard_map/ppermute | solution.py:291
  27.0 23.6 %collective-permute-start = (s32[64]{0:T(128)S(1)}, s32[64]{0:T(128)}, u32[]{:S(2)}, u32[]{:S(2)}) collective-permute-start(s32[64]{0:T(128)S(1)} %copy-done.7), channel_id=1, source_target_pairs={{0,1},{1,2},{2,3},{3,4},{4,5},{5,6},{6,7},{7,8},{8,9},{9,10},{10,1... | collective-permute-start | bytes 776 | tf_op jit(solution)/shard_map/ppermute | solution.py:337
  34.9 17.6 %collective-permute-start.1 = (s32[64]{0:T(128)S(1)}, s32[64]{0:T(128)}, u32[]{:S(2)}, u32[]{:S(2)}) collective-permute-start(s32[64]{0:T(128)S(1)} %copy-done.7), channel_id=1, source_target_pairs={{1,0},{2,1},{3,2},{4,3},{5,4},{6,5},{7,6},{8,7},{9,8},{10,9},{11,1... | collective-permute-start | bytes 776 | tf_op jit(solution)/shard_map/ppermute | solution.py:337
  36.8 102.2 %collective-permute-start.2 = (f32[3,64,128]{2,1,0:T(8,128)}, f32[3,64,128]{2,1,0:T(8,128)}, u32[]{:S(2)}, u32[]{:S(2)}) collective-permute-start(f32[3,64,128]{2,1,0:T(8,128)} %bitcast.3.p1), channel_id=1, source_target_pairs={{0,1},{1,2},{2,3},{3,4},{4,5},{5,6},{6,7},{7,8},{8,9},{9,10},{10,1... | collective-permute-start | bytes 294920 | tf_op jit(solution)/shard_map/ppermute | solution.py:335
  50.6 88.5 %collective-permute-start.3 = (f32[3,64,128]{2,1,0:T(8,128)}, f32[3,64,128]{2,1,0:T(8,128)}, u32[]{:S(2)}, u32[]{:S(2)}) collective-permute-start(f32[3,64,128]{2,1,0:T(8,128)} %bitcast.3.p1), channel_id=1, source_target_pairs={{1,0},{2,1},{3,2},{4,3},{5,4},{6,5},{7,6},{8,7},{9,8},{10,9},{11,1... | collective-permute-start | bytes 294920 | tf_op jit(solution)/shard_map/ppermute | solution.py:335
  52.5 4.0 %collective-permute-start.8 = (f32[32,152]{1,0:T(8,128)S(1)}, f32[32,152]{1,0:T(8,128)S(1)}, u32[]{:S(2)}, u32[]{:S(2)}) collective-permute-start(f32[32,152]{1,0:T(8,128)S(1)} %fusion.55), channel_id=1, source_target_pairs={{0,1},{1,0},{2,3},{3,2},{4,5},{5,4},{6,7},{7,6},{8,9},{9,8},{10,11... | collective-permute-start | bytes 58376 | tf_op jit(solution)/shard_map/ppermute | solution.py:299
  53.4 30.8 %copy-start.6 = (s32[192]{0:T(256)}, s32[192]{0:T(256)S(1)}, u32[]{:S(2)}) copy-start(s32[192]{0:T(256)S(1)} %pad_add_fusion.1.cnt) | copy-start | bytes 2308
  56.5 2.8 %collective-permute-start.9 = (f32[32,152]{1,0:T(8,128)S(1)}, f32[32,152]{1,0:T(8,128)S(1)}, u32[]{:S(2)}, u32[]{:S(2)}) collective-permute-start(f32[32,152]{1,0:T(8,128)S(1)} %add.259), channel_id=1, source_target_pairs={{0,2},{1,3},{2,0},{3,1},{4,6},{5,7},{6,4},{7,5},{8,10},{9,11},{10,... | collective-permute-start | bytes 58376 | tf_op jit(solution)/shard_map/ppermute | solution.py:299
  59.4 4.3 %collective-permute-start.10 = (f32[32,152]{1,0:T(8,128)S(1)}, f32[32,152]{1,0:T(8,128)S(1)}, u32[]{:S(2)}, u32[]{:S(2)}) collective-permute-start(f32[32,152]{1,0:T(8,128)S(1)} %add.260), channel_id=1, source_target_pairs={{0,4},{1,5},{2,6},{3,7},{4,0},{5,1},{6,2},{7,3},{8,12},{9,13},{10,... | collective-permute-start | bytes 58376 | tf_op jit(solution)/shard_map/ppermute | solution.py:299
  63.8 5.4 %collective-permute-start.11 = (f32[32,152]{1,0:T(8,128)S(1)}, f32[32,152]{1,0:T(8,128)S(1)}, u32[]{:S(2)}, u32[]{:S(2)}) collective-permute-start(f32[32,152]{1,0:T(8,128)S(1)} %fusion.52), channel_id=1, source_target_pairs={{0,8},{1,9},{2,10},{3,11},{4,12},{5,13},{6,14},{7,15},{8,0},{9,1},... | collective-permute-start | bytes 58376 | tf_op jit(solution)/shard_map/ppermute | solution.py:299
  69.3 69.8 %collective-permute-start.4 = (f32[64,32,128]{2,1,0:T(8,128)}, f32[64,32,128]{2,1,0:T(8,128)}, u32[]{:S(2)}, u32[]{:S(2)}) collective-permute-start(f32[64,32,128]{2,1,0:T(8,128)} %d1.1), channel_id=1, source_target_pairs={{0,1},{1,2},{2,3},{3,4},{4,5},{5,6},{6,7},{7,8},{8,9},{9,10},{10,1... | collective-permute-start | bytes 3145736 | tf_op jit(solution)/shard_map/ppermute | solution.py:336
  79.4 59.6 %collective-permute-start.5 = (f32[64,32,128]{2,1,0:T(8,128)}, f32[64,32,128]{2,1,0:T(8,128)}, u32[]{:S(2)}, u32[]{:S(2)}) collective-permute-start(f32[64,32,128]{2,1,0:T(8,128)} %d1.1), channel_id=1, source_target_pairs={{1,0},{2,1},{3,2},{4,3},{5,4},{6,5},{7,6},{8,7},{9,8},{10,9},{11,1... | collective-permute-start | bytes 3145736 | tf_op jit(solution)/shard_map/ppermute | solution.py:336
  82.7 9.6 %collective-permute-start.12 = (f32[32,152]{1,0:T(8,128)S(1)}, f32[32,152]{1,0:T(8,128)}, u32[]{:S(2)}, u32[]{:S(2)}) collective-permute-start(f32[32,152]{1,0:T(8,128)S(1)} %add.263), channel_id=1, source_target_pairs={{0,16},{1,17},{2,18},{3,19},{4,20},{5,21},{6,22},{7,23},{8,24},{9,... | collective-permute-start | bytes 58376 | tf_op jit(solution)/shard_map/ppermute | solution.py:299
  93.0 33.5 %collective-permute-start.13 = (f32[32,152]{1,0:T(8,128)S(1)}, f32[32,152]{1,0:T(8,128)S(1)}, u32[]{:S(2)}, u32[]{:S(2)}) collective-permute-start(f32[32,152]{1,0:T(8,128)S(1)} %add.264), channel_id=1, source_target_pairs={{0,32},{1,33},{2,34},{3,35},{4,36},{5,37},{6,38},{7,39},{8,40},{9,... | collective-permute-start | bytes 58376 | tf_op jit(solution)/shard_map/ppermute | solution.py:299
  126.7 4.3 %collective-permute-start.14 = (f32[32,152]{1,0:T(8,128)S(1)}, f32[32,152]{1,0:T(8,128)S(1)}, u32[]{:S(2)}, u32[]{:S(2)}) collective-permute-start(f32[32,152]{1,0:T(8,128)S(1)} %fusion.48), channel_id=1, source_target_pairs={{0,64},{1,65},{2,66},{3,67},{4,68},{5,69},{6,70},{7,71},{8,72},{9,... | collective-permute-start | bytes 58376 | tf_op jit(solution)/shard_map/ppermute | solution.py:299
  134.0 1.9 copy-start.4

commit v2 on v1

--- a/solution.py
+++ b/solution.py
@@ -280,31 +280,162 @@
     return sel, nodes
 
 
-def extended(value, sides, width):
-    for axis, dim in sides:
-        count, length = (lax.axis_size(axis), value.shape[dim])
-        up = [(i, (i + 1) % count) for i in range(count - 1)]
-        down = [(j, i) for i, j in up]
-        last = lax.slice_in_dim(value, length - width, length, axis=dim)
-        first = lax.slice_in_dim(value, 0, width, axis=dim)
-        before = lax.ppermute(last, axis, up)
-        after = lax.ppermute(first, axis, down)
-        value = jnp.concatenate([before, value, after], axis=dim)
-    return value
-
-
-def swapped(value, axis, bit):
-    mask = 2**bit
-    pairs = [(source, source ^ mask) for source in range(lax.axis_size(axis))]
-    return lax.ppermute(value, axis, pairs)
-
-
-def kernel(left_pts, right_pts):
-    total_sq = jnp.zeros((left_pts.shape[1], right_pts.shape[1]), jnp.float32)
-    for coord_index in range(3):
-        offset = left_pts[coord_index][:, None] - right_pts[coord_index][None, :]
-        total_sq = total_sq + offset * offset
-    return jnp.exp(-0.5 * total_sq)
+def dot3(a, b):
+    ah, al = split2(a)
+    bh, bl = split2(b)
+    left = jnp.concatenate([ah, al], axis=0)
+    r = jnp.dot(left, bh, preferred_element_type=F32)
+    m = a.shape[0]
+    return r[:m] + (r[m:] + jnp.dot(ah, bl, preferred_element_type=F32))
+
+
+def up_kernel(
+    pts, dens, surf, up_inv, shift_up, coarse,
+    pts_lo, pts_hi, dens_lo, dens_hi, nodes, slab,
+    check, node, near_top, far_top, send, recv,
+):
+    leaves, q_width = dens.shape[0], dens.shape[1]
+    width = up_inv.shape[0]
+    count = lax.axis_size("oct")
+    me = lax.axis_index("oct")
+    right = lax.rem(me + 1, count)
+    left = lax.rem(me + count - 1, count)
+    child = lax.rem(me, 8)
+    row = me // 8
+    rows = count // 8
+    mates = [me - child + lax.rem(child + k, 8) for k in range(1, 8)]
+    cousins = [lax.rem(row + k, rows) * 8 + child for k in range(1, rows)]
+
+    barrier = pltpu.get_barrier_semaphore()
+    for other in [left, right] + mates + cousins:
+        pl.semaphore_signal(barrier, inc=1, device_id=(other,), device_id_type=pl.DeviceIdType.MESH)
+    pl.semaphore_wait(barrier, 2 + len(mates) + len(cousins))
+
+    def push(src, dst, sem, device):
+        copy = pltpu.make_async_remote_copy(
+            src_ref=src, dst_ref=dst, send_sem=send.at[sem], recv_sem=recv.at[sem],
+            device_id=(device,), device_id_type=pl.DeviceIdType.MESH,
+        )
+        copy.start()
+        return copy
+
+    halo = [
+        push(pts, pts_lo, 0, right),
+        push(pts, pts_hi, 1, left),
+        push(dens, dens_lo, 2, right),
+        push(dens, dens_hi, 3, left),
+    ]
+
+    lane = lax.broadcasted_iota(jnp.int32, (32, 128), 1).astype(F32)
+    lane_big = lax.broadcasted_iota(jnp.int32, (128, 128), 1)
+
+    def leaf_group(g, carry):
+        tiles = []
+        for i in range(4):
+            tiles += source_tiles([pts[c, pl.ds(4 * g + i, 1), :] for c in range(3)])
+        turned = jnp.concatenate(tiles, axis=0).astype(BF).T
+        for i in range(4):
+            j = 4 * g + i
+            own = (lane_big >= 32 * i) & (lane_big < 32 * i + 32)
+            f = jnp.where(own, turned, jnp.zeros_like(turned))
+            w = jnp.concatenate(
+                [
+                    jnp.concatenate(
+                        target_tiles([surf[3 * h + c, pl.ds(j, 1), :] for c in range(3)]), axis=0
+                    ).astype(BF)
+                    for h in range(2)
+                ],
+                axis=1,
+            )
+            k = jnp.exp2(jnp.dot(f, jnp.concatenate([w] * 4, axis=0), preferred_element_type=F32))
+            hi, lo = split2(k)
+            used = jnp.broadcast_to(pts[3, pl.ds(j, 1), :], (32, 128))
+            mh, ml = split2(jnp.where(lane < used, dens[j], 0.0))
+            r = jnp.dot(
+                jnp.concatenate([mh, ml], axis=0), jnp.concatenate([hi, lo], axis=1), preferred_element_type=F32
+            )
+            c = 4 * lax.rem(g, 2) + i
+            n = g // 2
+            check[c, pl.ds(pl.multiple_of(32 * n, 32), 32), :] = (r[:32, :256] + r[:32, 256:]) + (
+                r[32:, :256] + r[32:, 256:]
+            )
+        return carry
+
+    lax.fori_loop(0, leaves // 4, leaf_group, 0)
+    node[...] = jnp.zeros_like(node)
+
+    def merge(c, carry):
+        both = dot3(up_inv[...], shift_up[c])
+        node[...] += dot3(check[c][:, :width], both)
+        return carry
+
+    lax.fori_loop(0, 8, merge, 0)
+    nodes[1] = node[...].astype(BF)
+    halo.append(push(nodes.at[1], nodes.at[0], 4, right))
+    halo.append(push(nodes.at[1], nodes.at[2], 5, left))
+
+    def climb(c, total):
+        return total + dot3(node[pl.ds(pl.multiple_of(32 * c, 32), 32), :], shift_up[c])
+
+    top = lax.fori_loop(0, 8, climb, jnp.zeros((q_width, width), F32))
+    near_top[0] = dot3(top, shift_up[child])
+    copies = [push(near_top.at[0], near_top.at[k], 5 + k, mates[k - 1]) for k in range(1, 8)]
+    for copy in copies:
+        copy.wait_recv()
+    top1 = near_top[0]
+    for k in range(1, 8):
+        top1 = top1 + near_top[k]
+    far_top[0] = top1
+    more = [push(far_top.at[0], far_top.at[k], 12 + k, cousins[k - 1]) for k in range(1, rows)]
+    total = dot3(top1, coarse[child])
+    for copy in more:
+        copy.wait_recv()
+    half = row // 8
+    own = jnp.zeros((q_width, width), F32)
+    other = jnp.zeros((q_width, width), F32)
+    for k in range(8):
+        src = lax.rem(row + rows - k, rows)
+        pair = dot3(jnp.concatenate([far_top[k], far_top[k + 8]], axis=0), shift_up[lax.rem(src, 8)])
+        same = jnp.where(src // 8 == half, 1.0, 0.0)
+        a, b = pair[:q_width], pair[q_width:]
+        own = own + (same * a + (1.0 - same) * b)
+        other = other + ((1.0 - same) * a + same * b)
+    top3 = dot3(own, shift_up[half]) + dot3(other, shift_up[1 - half])
+    total = total + dot3(own, coarse[lax.rem(row, 8)]) + dot3(top3, coarse[half])
+    slab[...] = total
+    for copy in halo:
+        copy.wait_recv()
+    for copy in halo + copies + more:
+        copy.wait_send()
+
+
+def up_call(pts, dens, surf, up_inv, shift_up, coarse):
+    leaves, q_width, _ = dens.shape
+    width = up_inv.shape[0]
+    vmem = pl.BlockSpec(memory_space=pltpu.VMEM)
+    hbm = pl.BlockSpec(memory_space=pl.ANY)
+    like = jax.ShapeDtypeStruct
+    return pl.pallas_call(
+        up_kernel,
+        out_shape=[
+            like(pts.shape, F32), like(pts.shape, F32), like(dens.shape, F32), like(dens.shape, F32),
+            like((3, 8 * q_width, width), BF), like((q_width, width), F32),
+        ],
+        in_specs=[vmem] * 6,
+        out_specs=[hbm] * 4 + [vmem] * 2,
+        scratch_shapes=[
+            pltpu.VMEM((8, 8 * q_width, 256), F32),
+            pltpu.VMEM((8 * q_width, width), F32),
+            pltpu.VMEM((8, q_width, width), F32),
+            pltpu.VMEM((16, q_width, width), F32),
+            pltpu.SemaphoreType.DMA((28,)),
+            pltpu.SemaphoreType.DMA((28,)),
+        ],
+        compiler_params=pltpu.CompilerParams(
+            vmem_limit_bytes=48 * 1024 * 1024, collective_id=0, has_side_effects=True
+        ),
+        name="upward",
+    )(pts, dens, surf, up_inv, shift_up, coarse)
 
 
 def local(
@@ -325,45 +456,22 @@
     eq_width = surface.shape[2]
     node_count = vlist.shape[0]
     index = lax.axis_index("oct")
-    slots = jnp.arange(p_width)
-    mask = (slots[None, :] < counts[:, None]).astype(jnp.float32)[:, None, :]
-    masked = dens * mask
-    count = lax.axis_size("oct")
-    up = [(i, (i + 1) % count) for i in range(count - 1)]
-    down = [(i, j) for j, i in up]
-    turned_points = jnp.transpose(points, (1, 0, 2))
-    points3 = [lax.ppermute(turned_points, "oct", up), turned_points, lax.ppermute(turned_points, "oct", down)]
-    dens3 = [lax.ppermute(dens, "oct", up), dens, lax.ppermute(dens, "oct", down)]
-    counts3 = jnp.concatenate([lax.ppermute(counts, "oct", up), counts, lax.ppermute(counts, "oct", down)])
+    turned_points = jnp.concatenate(
+        [
+            jnp.transpose(points, (1, 0, 2)),
+            jnp.broadcast_to(counts.astype(F32)[None, :, None], (1, leaf_count, p_width)),
+        ],
+        axis=0,
+    )
+    surf = jnp.pad(jnp.transpose(surface, (1, 0, 2)), ((0, 0), (0, 0), (0, 256 - eq_width)))
+    surf = jnp.concatenate([surf[:, :, :128], surf[:, :, 128:]], axis=0)
+    points_lo, points_hi, dens_lo, dens_hi, cycle, slab_local = up_call(
+        turned_points, dens, surf, up_inverse, shift_up, coarse
+    )
+    points3 = [points_lo, turned_points, points_hi]
+    dens3 = [dens_lo, dens, dens_hi]
+    counts3 = jnp.concatenate([p[3, :, 0] for p in points3]).astype(jnp.int32)
     lists = make_lists(ulist, counts3, (index - 1) * leaf_count)
-    up_kernel = jax.vmap(kernel)(points, surface)
-    check = jnp.einsum("lqp,lpe->lqe", masked, up_kernel, precision=HIGHEST)
-    leaf_eq = jnp.dot(
-        check.reshape(-1, eq_width),
-        up_inverse,
-        precision=HIGHEST,
-        preferred_element_type=jnp.float32,
-    ).reshape(leaf_count, q_width, eq_width)
-    node_eq = jnp.einsum(
-        "ncqe,cef->nqf", leaf_eq.reshape(-1, 8, q_width, eq_width), shift_up, precision=HIGHEST
-    )
-    node_send = node_eq.astype(jnp.bfloat16).reshape(node_count, q_width * eq_width)
-    slab_eq = jnp.einsum("cqe,cef->qf", node_eq, shift_up, precision=HIGHEST)
-    cycle = extended(node_send, (("oct", 0),), node_count)
-    bit_count = lax.axis_size("oct").bit_length() - 1
-    slab_local = jnp.zeros((q_width, eq_width), jnp.float32)
-    current = slab_eq
-    for level_start in range(0, bit_count, 3):
-        width_bits = min(3, bit_count - level_start)
-        child_slot = jnp.right_shift(index, level_start) & 7
-        current = jnp.dot(
-            current, shift_up[child_slot], precision=HIGHEST, preferred_element_type=jnp.float32
-        )
-        for bit_number in range(level_start, level_start + width_bits):
-            current = current + swapped(current, "oct", bit_number)
-        slab_local = slab_local + jnp.dot(
-            current, coarse[child_slot], precision=HIGHEST, preferred_element_type=jnp.float32
-        )
     cycle = cycle.reshape(3 * node_count, q_width, eq_width)
     sel, nodes = far_inputs(vlist, (index - 1) * node_count, cycle)
     far_node = far_call(jnp.transpose(translate, (1, 2, 0)), sel, nodes)
@@ -381,8 +489,6 @@
         precision=HIGHEST,
         preferred_element_type=jnp.float32,
     ).reshape(leaf_count, q_width, wide)
-    surf = jnp.pad(jnp.transpose(surface, (1, 0, 2)), ((0, 0), (0, 0), (0, pad)))
-    surf = jnp.concatenate([surf[:, :, :128], surf[:, :, 128:]], axis=0)
     return near_call(counts3, *lists, points3, dens3, surf, leaf_down)
 
 

time: 188 us -> 135 us (0.72)
  the two profiles are of different devices: /device:TPU:31 before, /device:TPU:1 now
where the time goes in v2:
time: 135 us; the launch traced here: 134 us
  Pallas kernels  108 us (80%)
  local copies, waits for them, and re-layouts  10.1 us (7%)
  other arithmetic  8.63 us (6%)
  matrix products  5.74 us (4%)
    pallas_call x1, Pallas kernels, near_call(): pl.pallas_call(functools.partial(near_kernel, leaves), out_shape=jax.Shap...  48.7 us
    pallas_call x1, Pallas kernels, up_call(): pl.pallas_call(up_kernel, out_shape=[like(pts.shape, F32), like(pts.shape...  38 us
    pallas_call x1, Pallas kernels, far_call(): pl.pallas_call(lambda *refs: far_kernel(step, *refs), grid=(count // step...  21.8 us
    unnamed x24, local copies, waits for them, and re-layouts  4.19 us
    dot_general x1, matrix products, local(): jnp.dot(leaf_local.reshape(-1, eq_width), jnp.pad(down_inverse, ((0, 0),...  3.14 us

profile of v2, /device:TPU:1, one launch (start us, length us, event | category | flops | bytes accessed | tf_op | source)
XLA Modules:
  0.0 133.9 jit_solution(378665801863295618)
XLA Ops:
  0.0 0.8 convert_element_type.16
  0.9 0.7 select_bitcast_fusion
  1.7 0.7 broadcast_multiply_fusion
  2.4 0.9 pad_maximum_fusion.1.pts.p1
  3.4 1.0 fusion.30
  4.7 1.3 copy-done.3
  5.9 0.9 copy-done.9
  6.9 38.0 %upward.1 = (f32[4,64,128]{2,1,0:T(8,128)S(1)}, f32[4,64,128]{2,1,0:T(8,128)S(1)}, f32[64,32,128]{2,1,0:T(8,128)S(1)}, f32[64,32,128]{2,1,0:T(8,128)S(1)}, bf16[...) custom-call(f32[4,64,128]{2,1,0:T(8,128)S(1)} %pad_maximum_fusion.1.pts.p1, f32[64,32,128]{2,1,0:T(8,128)S(1)} %copy-done.1, ...), custom_call_target="tpu_custom_call" | custom-call | tf_op jit(solution)/shard_map/upward/pallas_call | solution.py:418
  44.9 1.0 copy-done.5
  45.9 1.0 copy-done.6
  47.1 0.8 select_reduce_fusion
  48.0 0.6 slice.22
  49.5 1.0 select_reduce_fusion.1
  50.5 0.8 select_reduce_fusion.3
  51.3 1.2 fusion.27.ptr
  52.8 1.1 copy.31
  53.9 1.5 %reshape.238 = s32[16384]{0:T(1024)S(1)} reshape(s32[64,16,2,8]{3,2,1,0:T(2,128)S(1)} %copy.31) | data formatting | bytes 131072 | tf_op jit(solution)/shard_map/reshape | solution.py:219
  55.4 0.6 concatenate.18.units
  56.5 1.0 fusion.6.refs_2_
  57.5 21.8 %far.1 = f32[152,256]{1,0:T(8,128)S(1)} custom-call(bf16[152,152,316]{2,1,0:T(8,128)(2,1)} %bitcast.42, bf16[316,256]{1,0:T(8,128)(2,1)S(1)} %compare_convert_fusion.refs_1_, bf16[152,32,128]{2,1,0:T(8,128)(2,1)S(1)} %fusion.6.refs_2_), custom_call_target="tpu_custom_call" | custom-call | tf_op jit(solution)/shard_map/far/pallas_call | solution.py:260
  79.4 0.8 fusion.10
  80.2 1.8 %fusion.7 = f32[8,32,8,152]{3,1,2,0:T(8,128)S(1)} fusion(f32[8,32,152,1]{2,1,3,0:T(8,128)S(1)} %fusion.10, f32[8,152,152]{2,1,0:T(8,128)S(1)} %copy-done), kind=kOutput, calls=%fused_computation.10 | convolution fusion | flops 567803904 | bytes 2140160 | tf_op jit(solution)/shard_map/nqe,cef->ncqf/dot_general | solution.py:481
  82.1 3.1 %fusion.15.down = f32[64,32,256]{2,1,0:T(8,128)} fusion(f32[64,32,152]{2,1,0:T(8,128)S(1)} %bitcast.43, f32[152,152]{1,0:T(8,128)S(1)} %copy-done.10), kind=kOutput, calls=%fused_computation.29 | convolution fusion | flops 956301312 | bytes 3434752 | tf_op jit(solution)/shard_map/dot_general | solution.py:486
  85.2 48.7 %near.1 = f32[64,32,128]{2,1,0:T(8,128)} custom-call(s32[192]{0:T(256)} %copy-done.11, s32[16400]{0:T(1024)} %concatenate.18.units, s32[1040]{0:T(1024)} %fusion.27.ptr, s32[1040]{0:T(1024)} %get-tuple-element.17.leaf, s32[1]{0:T(128)} %bitcast.4.total_ref, f32[4,64,128]{2,1,0:T(8,128)} %copy-done.7, f32[4,64,128]{2,1,0:T(8,128)} %copy-done.4, ...), custom_call_target="tpu_custom_call" | custom-call | tf_op jit(solution)/shard_map/near/pallas_call | solution.py:176
  (46 shorter events, 1.8 us)
Async XLA Ops:
  0.0 79.4 %copy-start = (f32[8,152,152]{2,1,0:T(8,128)S(1)}, f32[8,152,152]{2,1,0:T(8,128)}, u32[]{:S(2)}) copy-start(f32[8,152,152]{2,1,0:T(8,128)} %param.21) | copy-start | bytes 2217988
  0.0 4.6 %copy-start.1 = (f32[64,32,128]{2,1,0:T(8,128)S(1)}, f32[64,32,128]{2,1,0:T(8,128)}, u32[]{:S(2)}) copy-start(f32[64,32,128]{2,1,0:T(8,128)} %d1.1) | copy-start | bytes 3145732
  3.4 41.5 %copy-start.4 = (f32[4,64,128]{2,1,0:T(8,128)}, f32[4,64,128]{2,1,0:T(8,128)S(1)}, u32[]{:S(2)}) copy-start(f32[4,64,128]{2,1,0:T(8,128)S(1)} %pad_maximum_fusion.1.pts.p1) | copy-start | bytes 393220
  4.4 40.5 %copy-start.2 = (f32[6,64,128]{2,1,0:T(8,128)}, f32[6,64,128]{2,1,0:T(8,128)S(1)}, u32[]{:S(2)}) copy-start(f32[6,64,128]{2,1,0:T(8,128)S(1)} %pad_maximum_fusion.surf) | copy-start | bytes 589828
  4.6 1.3 copy-start.3
  5.9 0.9 copy-start.9
  44.9 1.0 copy-start.5
  45.9 1.0 copy-start.6
  46.9 9.6 %copy-start.7 = (f32[4,64,128]{2,1,0:T(8,128)}, f32[4,64,128]{2,1,0:T(8,128)S(1)}, u32[]{:S(2)}) copy-start(f32[4,64,128]{2,1,0:T(8,128)S(1)} %get-tuple-element.11.p0) | copy-start | bytes 393220
  46.9 9.7 %copy-start.8 = (f32[4,64,128]{2,1,0:T(8,128)}, f32[4,64,128]{2,1,0:T(8,128)S(1)}, u32[]{:S(2)}) copy-start(f32[4,64,128]{2,1,0:T(8,128)S(1)} %get-tuple-element.12.p2) | copy-start | bytes 393220
  47.1 9.5 %copy-start.11 = (s32[192]{0:T(256)}, s32[192]{0:T(256)S(1)}, u32[]{:S(2)}) copy-start(s32[192]{0:T(256)S(1)} %maximum_convert_fusion.cnt) | copy-start | bytes 2308
  80.2 1.9 %copy-start.10 = (f32[152,152]{1,0:T(8,128)S(1)}, f32[152,152]{1,0:T(8,128)}, u32[]{:S(2)}) copy-start(f32[152,152]{1,0:T(8,128)} %param.19) | copy-start | bytes 277252

commit v3 on v2

--- a/solution.py
+++ b/solution.py
@@ -7,7 +7,6 @@
 from jax.experimental.pallas import tpu as pltpu
 from jax.sharding import PartitionSpec as P
 
-HIGHEST = lax.Precision.HIGHEST
 BF = jnp.bfloat16
 F32 = jnp.float32
 LIST = 128
@@ -222,64 +221,6 @@
     return [v.astype(jnp.int32) for v in (both, ptr, leaf, rounds)]
 
 
-def far_kernel(step, table, sel, nodes, out):
-    width = table.shape[1]
-    lane = lax.broadcasted_iota(jnp.int32, (32, 128), 1)
-
-    @pl.when(pl.program_id(0) == 0)
-    def _():
-        out[...] = jnp.zeros_like(out)
-
-    zero = jnp.zeros((32, 128), BF)
-    picks = sel[...]
-    total = None
-    for k in range(0, step, 2):
-        sums = []
-        for e in (k, k + 1):
-            s = jnp.dot(table[e], picks, preferred_element_type=F32)
-            hi, lo = split2(s)
-            sums.append(jnp.concatenate([hi, lo], axis=0))
-        rows = []
-        for e in (k, k + 1):
-            x = nodes[e]
-            for n in range(8):
-                own = (lane >= 32 * (n % 4)) & (lane < 32 * (n % 4) + 32)
-                part = jnp.where(own, x, zero)
-                rows.append(jnp.concatenate([part, zero] if n < 4 else [zero, part], axis=1))
-        r = jnp.dot(
-            jnp.concatenate(sums, axis=1), jnp.concatenate(rows, axis=0), preferred_element_type=F32
-        )
-        r = r[:width] + r[width:]
-        total = r if total is None else total + r
-    out[...] += total
-
-
-def far_call(table, sel, nodes):
-    count, width, types = table.shape
-    step = 8
-    return pl.pallas_call(
-        lambda *refs: far_kernel(step, *refs),
-        grid=(count // step,),
-        out_shape=jax.ShapeDtypeStruct((width, 256), F32),
-        in_specs=[
-            pl.BlockSpec((step, width, types), lambda i: (i, 0, 0)),
-            pl.BlockSpec((types, 256), lambda i: (0, 0)),
-            pl.BlockSpec((step, 32, 128), lambda i: (i, 0, 0)),
-        ],
-        out_specs=pl.BlockSpec((width, 256), lambda i: (0, 0)),
-        compiler_params=pltpu.CompilerParams(vmem_limit_bytes=48 * 1024 * 1024),
-        name="far",
-    )(table, sel, nodes)
-
-
-def far_inputs(vlist, base, cycle):
-    rel = jnp.where(vlist >= 0, vlist - base, -1)
-    sel = (rel.T[:, :, None] == jnp.arange(32)).astype(BF).reshape(rel.shape[1], 256)
-    turned = jnp.transpose(cycle, (2, 0, 1))
-    nodes = jnp.pad(jnp.concatenate([turned] * 4, axis=2), ((0, 0), (0, 8), (0, 0)))
-    return sel, nodes
-
-
 def dot3(a, b):
     ah, al = split2(a)
     bh, bl = split2(b)
@@ -290,9 +231,9 @@
 
 
 def up_kernel(
-    pts, dens, surf, up_inv, shift_up, coarse,
-    pts_lo, pts_hi, dens_lo, dens_hi, nodes, slab,
-    check, node, near_top, far_top, send, recv,
+    pts, dens, surf, sel, up_inv, down_inv, shift_up, shift_down, coarse, table,
+    pts_lo, pts_hi, dens_lo, dens_hi, down,
+    check, node, nodes, near_top, far_top, held, sources, far_sum, send, recv, table_sem,
 ):
     leaves, q_width = dens.shape[0], dens.shape[1]
     width = up_inv.shape[0]
@@ -306,6 +247,16 @@
     mates = [me - child + lax.rem(child + k, 8) for k in range(1, 8)]
     cousins = [lax.rem(row + k, rows) * 8 + child for k in range(1, rows)]
 
+    def fetch(b):
+        part = pl.ds(pl.multiple_of(STEP * b, STEP), STEP)
+        return pltpu.make_async_copy(table.at[part], held.at[part], table_sem.at[b])
+
+    def fetch_start(b, carry):
+        fetch(b).start()
+        return carry
+
+    blocks = held.shape[0] // STEP
+    lax.fori_loop(0, blocks, fetch_start, 0)
     barrier = pltpu.get_barrier_semaphore()
     for other in [left, right] + mates + cousins:
         pl.semaphore_signal(barrier, inc=1, device_id=(other,), device_id_type=pl.DeviceIdType.MESH)
@@ -363,6 +314,8 @@
 
     lax.fori_loop(0, leaves // 4, leaf_group, 0)
     node[...] = jnp.zeros_like(node)
+    far_sum[...] = jnp.zeros_like(far_sum)
+    down[...] = jnp.zeros_like(down)
 
     def merge(c, carry):
         both = dot3(up_inv[...], shift_up[c])
@@ -370,7 +323,7 @@
         return carry
 
     lax.fori_loop(0, 8, merge, 0)
-    nodes[1] = node[...].astype(BF)
+    nodes[1, :, :width] = node[...].astype(BF)
     halo.append(push(nodes.at[1], nodes.at[0], 4, right))
     halo.append(push(nodes.at[1], nodes.at[2], 5, left))
 
@@ -378,16 +331,38 @@
         return total + dot3(node[pl.ds(pl.multiple_of(32 * c, 32), 32), :], shift_up[c])
 
     top = lax.fori_loop(0, 8, climb, jnp.zeros((q_width, width), F32))
-    near_top[0] = dot3(top, shift_up[child])
+    near_top[0, :, :width] = dot3(top, shift_up[child])
     copies = [push(near_top.at[0], near_top.at[k], 5 + k, mates[k - 1]) for k in range(1, 8)]
+
+    def turn(slab):
+        x = nodes[slab].astype(F32)
+        for i in range(8):
+            rows32 = x[32 * i : 32 * i + 32]
+            turned = jnp.concatenate([rows32] * 4, axis=0).T
+            sources[slab, :, i, :] = turned[:width]
+
+    turn(1)
+    for copy in halo[4:]:
+        copy.wait_recv()
+    turn(0)
+    turn(2)
+    picks = sel[...]
+
+    def far_block(b, carry):
+        fetch(b).wait()
+        far_sum[:width, :] += far_step(lambda k: held[STEP * b + k], picks, lambda k: [sources[h, STEP * b + k] for h in range(3)], width)
+        return carry
+
+    lax.fori_loop(0, blocks // 3, far_block, 0)
     for copy in copies:
         copy.wait_recv()
-    top1 = near_top[0]
+    top1 = near_top[0, :, :width]
     for k in range(1, 8):
-        top1 = top1 + near_top[k]
-    far_top[0] = top1
+        top1 = top1 + near_top[k, :, :width]
+    far_top[0, :, :width] = top1
     more = [push(far_top.at[0], far_top.at[k], 12 + k, cousins[k - 1]) for k in range(1, rows)]
     total = dot3(top1, coarse[child])
+    lax.fori_loop(blocks // 3, 2 * blocks // 3, far_block, 0)
     for copy in more:
         copy.wait_recv()
     half = row // 8
@@ -395,47 +370,96 @@
     other = jnp.zeros((q_width, width), F32)
     for k in range(8):
         src = lax.rem(row + rows - k, rows)
-        pair = dot3(jnp.concatenate([far_top[k], far_top[k + 8]], axis=0), shift_up[lax.rem(src, 8)])
+        pair = dot3(jnp.concatenate([far_top[k, :, :width], far_top[k + 8, :, :width]], axis=0), shift_up[lax.rem(src, 8)])
         same = jnp.where(src // 8 == half, 1.0, 0.0)
         a, b = pair[:q_width], pair[q_width:]
         own = own + (same * a + (1.0 - same) * b)
         other = other + ((1.0 - same) * a + same * b)
     top3 = dot3(own, shift_up[half]) + dot3(other, shift_up[1 - half])
     total = total + dot3(own, coarse[lax.rem(row, 8)]) + dot3(top3, coarse[half])
-    slab[...] = total
-    for copy in halo:
+    lax.fori_loop(2 * blocks // 3, blocks, far_block, 0)
+    node[...] = far_sum[...].T[:, :width]
+
+    def parent(c, carry):
+        at = pl.ds(pl.multiple_of(32 * c, 32), 32)
+        node[at, :] = node[at, :] + dot3(total, shift_down[c])
+        return carry
+
+    lax.fori_loop(0, 8, parent, 0)
+
+    def descend(c, carry):
+        leaf = dot3(node[...], dot3(shift_down[c], down_inv[...]))
+        for n in range(8):
+            down[8 * n + c, :, :width] = leaf[32 * n : 32 * n + 32]
+        return carry
+
+    lax.fori_loop(0, 8, descend, 0)
+    for copy in halo[:4]:
         copy.wait_recv()
     for copy in halo + copies + more:
         copy.wait_send()
 
 
-def up_call(pts, dens, surf, up_inv, shift_up, coarse):
+STEP = 8
+
+
+def far_step(table_at, picks, rows_at, width):
+    lane = lax.broadcasted_iota(jnp.int32, (32, 128), 1)
+    zero = jnp.zeros((32, 128), BF)
+    total = None
+    for k in range(0, STEP, 2):
+        sums = []
+        rows = []
+        for e in (k, k + 1):
+            s = jnp.dot(table_at(e), picks, preferred_element_type=F32)
+            hi, lo = split2(s)
+            sums.append(jnp.concatenate([hi, lo], axis=0))
+            x = jnp.concatenate(rows_at(e) + [jnp.zeros((8, 128), F32)], axis=0).astype(BF)
+            for n in range(8):
+                own = (lane >= 32 * (n % 4)) & (lane < 32 * (n % 4) + 32)
+                part = jnp.where(own, x, zero)
+                rows.append(jnp.concatenate([part, zero] if n < 4 else [zero, part], axis=1))
+        r = jnp.dot(
+            jnp.concatenate(sums, axis=1), jnp.concatenate(rows, axis=0), preferred_element_type=F32
+        )
+        r = r[:width] + r[width:]
+        total = r if total is None else total + r
+    return total
+
+
+def up_call(pts, dens, surf, sel, up_inv, down_inv, shift_up, shift_down, coarse, table):
     leaves, q_width, _ = dens.shape
     width = up_inv.shape[0]
     vmem = pl.BlockSpec(memory_space=pltpu.VMEM)
     hbm = pl.BlockSpec(memory_space=pl.ANY)
     like = jax.ShapeDtypeStruct
+    rows = 8 * q_width
     return pl.pallas_call(
         up_kernel,
         out_shape=[
             like(pts.shape, F32), like(pts.shape, F32), like(dens.shape, F32), like(dens.shape, F32),
-            like((3, 8 * q_width, width), BF), like((q_width, width), F32),
+            like((leaves, q_width, 256), F32),
         ],
-        in_specs=[vmem] * 6,
-        out_specs=[hbm] * 4 + [vmem] * 2,
+        in_specs=[vmem] * 9 + [hbm],
+        out_specs=[hbm] * 4 + [vmem],
         scratch_shapes=[
-            pltpu.VMEM((8, 8 * q_width, 256), F32),
-            pltpu.VMEM((8 * q_width, width), F32),
-            pltpu.VMEM((8, q_width, width), F32),
-            pltpu.VMEM((16, q_width, width), F32),
+            pltpu.VMEM((8, rows, 256), F32),
+            pltpu.VMEM((rows, width), F32),
+            pltpu.VMEM((3, rows, 256), BF),
+            pltpu.VMEM((8, q_width, 256), F32),
+            pltpu.VMEM((16, q_width, 256), F32),
+            pltpu.VMEM(table.shape, BF),
+            pltpu.VMEM((3, width, 8, 128), F32),
+            pltpu.VMEM((256, rows), F32),
             pltpu.SemaphoreType.DMA((28,)),
             pltpu.SemaphoreType.DMA((28,)),
+            pltpu.SemaphoreType.DMA((table.shape[0] // STEP,)),
         ],
         compiler_params=pltpu.CompilerParams(
-            vmem_limit_bytes=48 * 1024 * 1024, collective_id=0, has_side_effects=True
+            vmem_limit_bytes=56 * 1024 * 1024, collective_id=0, has_side_effects=True
         ),
         name="upward",
-    )(pts, dens, surf, up_inv, shift_up, coarse)
+    )(pts, dens, surf, sel, up_inv, down_inv, shift_up, shift_down, coarse, table)
 
 
 def local(
@@ -465,30 +489,16 @@
     )
     surf = jnp.pad(jnp.transpose(surface, (1, 0, 2)), ((0, 0), (0, 0), (0, 256 - eq_width)))
     surf = jnp.concatenate([surf[:, :, :128], surf[:, :, 128:]], axis=0)
-    points_lo, points_hi, dens_lo, dens_hi, cycle, slab_local = up_call(
-        turned_points, dens, surf, up_inverse, shift_up, coarse
+    rel = jnp.where(vlist >= 0, vlist - (index - 1) * node_count, -1)
+    sel = (rel.T[:, :, None] == jnp.arange(32)).astype(BF).reshape(rel.shape[1], 256)
+    points_lo, points_hi, dens_lo, dens_hi, leaf_down = up_call(
+        turned_points, dens, surf, sel, up_inverse, down_inverse, shift_up, shift_down, coarse,
+        jnp.transpose(translate, (1, 2, 0)),
     )
     points3 = [points_lo, turned_points, points_hi]
     dens3 = [dens_lo, dens, dens_hi]
     counts3 = jnp.concatenate([p[3, :, 0] for p in points3]).astype(jnp.int32)
     lists = make_lists(ulist, counts3, (index - 1) * leaf_count)
-    cycle = cycle.reshape(3 * node_count, q_width, eq_width)
-    sel, nodes = far_inputs(vlist, (index - 1) * node_count, cycle)
-    far_node = far_call(jnp.transpose(translate, (1, 2, 0)), sel, nodes)
-    far_node = far_node.T.reshape(node_count, q_width, eq_width)
-    parent_part = jnp.einsum("qe,cef->cqf", slab_local, shift_down, precision=HIGHEST)
-    node_local = far_node + parent_part
-    leaf_local = jnp.einsum("nqe,cef->ncqf", node_local, shift_down, precision=HIGHEST).reshape(
-        leaf_count, q_width, eq_width
-    )
-    wide = 256
-    pad = wide - eq_width
-    leaf_down = jnp.dot(
-        leaf_local.reshape(-1, eq_width),
-        jnp.pad(down_inverse, ((0, 0), (0, pad))),
-        precision=HIGHEST,
-        preferred_element_type=jnp.float32,
-    ).reshape(leaf_count, q_width, wide)
     return near_call(counts3, *lists, points3, dens3, surf, leaf_down)
 
 

time: 135 us -> 121 us (0.90)
  matrix products: 5.74 us -> 0 us
  Pallas kernels: 108 us -> 103 us
  local copies, waits for them, and re-layouts: 10.1 us -> 6.05 us
    pallas_call x1 -> x0, Pallas kernels: 21.8 us -> none  [far_call(): pl.pallas_call(lambda *refs: far_kernel(step, *refs), grid=(count // step...]
    pallas_call x1, Pallas kernels: 38 us -> 58.4 us  [up_call(): pl.pallas_call(up_kernel, out_shape=[like(pts.shape, F32), like(pts.shape...]
    dot_general x3 -> x0, matrix products: 5.74 us -> none  [the longest x1 3.14 us: local(): jnp.dot(leaf_local.reshape(-1, eq_width), jnp.pad(down_inverse, ((0, 0),...]
    unnamed x24 -> x4, local copies, waits for them, and re-layouts: 4.19 us -> 0.01 us
    pallas_call x1, Pallas kernels: 48.7 us -> 45 us  [near_call(): pl.pallas_call(functools.partial(near_kernel, leaves), out_shape=jax.Shap...]
where the time goes in v3:
time: 121 us; the launch traced here: 119 us
  Pallas kernels  103 us (85%)
  other arithmetic  8.76 us (7%)
  local copies, waits for them, and re-layouts  6.05 us (5%)
    pallas_call x1, Pallas kernels, up_call(): pl.pallas_call(up_kernel, out_shape=[like(pts.shape, F32), like(pts.shape...  58.4 us
    pallas_call x1, Pallas kernels, near_call(): pl.pallas_call(functools.partial(near_kernel, leaves), out_shape=jax.Shap...  45 us

profile of v3, /device:TPU:1, one launch (start us, length us, event | category | flops | bytes accessed | tf_op | source)
XLA Modules:
  0.0 119.0 jit_solution(15757037959159082520)
XLA Ops:
  0.0 0.7 convert_element_type.12
  0.7 1.6 %pad_maximum_fusion.1.pts.p1 = f32[4,64,128]{2,1,0:T(8,128)} fusion(f32[1,64,128]{2,1,0:T(8,128)S(1)} %broadcast_in_dim.94, f32[3,64,128]{2,1,0:T(8,128)} %bitcast.14), kind=kLoop, calls=%fused_computation.16 | loop fusion | flops 32768 | bytes 262144 | tf_op jit(solution)/shard_map/concatenate | solution.py:483
  2.3 1.0 fusion.14
  3.2 0.7 pad_maximum_fusion.surf
  3.9 0.7 select_bitcast_fusion
  4.7 0.1 copy.26
  4.8 0.1 eq.39
  4.9 0.7 compare_convert_fusion.sel
  5.6 58.4 %upward.1 = (f32[4,64,128]{2,1,0:T(8,128)}, f32[4,64,128]{2,1,0:T(8,128)}, f32[64,32,128]{2,1,0:T(8,128)}, f32[64,32,128]{2,1,0:T(8,128)}, f32[64,32,256]{2,1,0:T(8,128)}) custom-call(f32[4,64,128]{2,1,0:T(8,128)} %pad_maximum_fusion.1.pts.p1, f32[64,32,128]{2,1,0:T(8,128)} %d1.1, f32[6,64,128]{2,1,0:T(8,128)} %pad_maximum_fusion.surf, ...), custom_call_target="tpu_custom_call" | custom-call | tf_op jit(solution)/shard_map/upward/pallas_call | solution.py:437
  64.1 0.9 slice_reduce_fusion
  64.9 0.1 maximum_convert_fusion.cnt
  65.1 0.8 select_reduce_fusion
  65.9 0.2 select_reduce_fusion.2
  66.1 1.0 select_reduce_fusion.1
  67.1 0.1 copy.27
  67.2 0.1 fusion.6
  67.4 1.1 copy.28
  68.5 1.5 %reshape.229 = s32[16384]{0:T(1024)S(1)} reshape(s32[64,16,2,8]{3,2,1,0:T(2,128)S(1)} %copy.28) | data formatting | bytes 131072 | tf_op jit(solution)/shard_map/reshape | solution.py:218
  70.0 0.6 concatenate.15.units
  70.6 0.1 select_reduce_fusion.5
  70.8 0.8 select_reduce_fusion.3
  71.5 0.6 slice.22
  72.1 1.2 %fusion.12.ptr = s32[1040]{0:T(1024)} fusion(s32[1040]{0:T(1024)S(1)} %get-tuple-element.16, s32[]{:T(128)} %bitcast.6), kind=kLoop, calls=%fused_computation.50 | loop fusion | flops 2080 | bytes 8324 | tf_op jit(solution)/shard_map/jit(_where)/select_n | solution.py:217
  74.0 45.0 %near.1 = f32[64,32,128]{2,1,0:T(8,128)} custom-call(s32[192]{0:T(256)} %copy-done.1, s32[16400]{0:T(1024)} %concatenate.15.units, s32[1040]{0:T(1024)} %fusion.12.ptr, s32[1040]{0:T(1024)} %get-tuple-element.15.leaf, s32[1]{0:T(128)} %bitcast.7.total_ref, f32[4,64,128]{2,1,0:T(8,128)} %get-tuple-element.10.p0, f32[4,64,128]{2,1,0:T(8,128)} %pad_maximum_fusion.1.pts.p1, ...), custom_call_target="tpu_custom_call" | custom-call | tf_op jit(solution)/shard_map/near/pallas_call | solution.py:175
  (19 shorter events, 0.2 us)
Async XLA Ops:
  5.6 59.4 %copy-start = (s32[64,27]{0,1:T(8,128)S(1)}, s32[64,27]{0,1:T(8,128)}, u32[]{:S(2)}) copy-start(s32[64,27]{0,1:T(8,128)} %param.16) | copy-start | bytes 20740
  65.0 9.0 %copy-start.1 = (s32[192]{0:T(256)}, s32[192]{0:T(256)S(1)}, u32[]{:S(2)}) copy-start(s32[192]{0:T(256)S(1)} %maximum_convert_fusion.cnt) | copy-start | bytes 2308

commit v4 on v3

v4 whole, which is shorter than its diff:
```python
import functools

import jax
import jax.numpy as jnp
from jax import lax
from jax.experimental import pallas as pl
from jax.experimental.pallas import tpu as pltpu
from jax.sharding import PartitionSpec as P

BF = jnp.bfloat16
F32 = jnp.float32


def split2(x):
    hi = x.astype(BF)
    lo = (x - hi.astype(F32)).astype(BF)
    return hi, lo


def split3(x):
    a = x.astype(BF).astype(F32)
    r = x - a
    b = r.astype(BF).astype(F32)
    return a, b, r - b


def rows8(shape):
    return lax.broadcasted_iota(jnp.int32, shape, 0)


LOG2E = 1.4426950408889634


def source_tiles(coords):
    out = []
    norm = None
    row = rows8((8, 128))
    for c in coords:
        x = jnp.broadcast_to(c, (8, 128))
        a, b, d = split3(LOG2E * x)
        first = (row <= 1) | (row == 4)
        out.append(jnp.where(first, a, jnp.where(row <= 3, b, jnp.where(row == 5, d, 0.0))))
        norm = x * x if norm is None else norm + x * x
    a, b, d = split3((-0.5 * LOG2E) * norm)
    out.append(
        jnp.where(row == 0, a, jnp.where(row == 1, b, jnp.where(row == 2, d, jnp.where(row <= 5, 1.0, 0.0))))
    )
    return out


def target_tiles(coords):
    out = []
    norm = None
    row = rows8((8, 128))
    for c in coords:
        x = jnp.broadcast_to(c, (8, 128))
        a, b, d = split3(x)
        first = (row == 0) | (row == 2) | (row == 5)
        second = (row == 1) | (row == 3)
        out.append(jnp.where(first, a, jnp.where(second, b, jnp.where(row == 4, d, 0.0))))
        norm = x * x if norm is None else norm + x * x
    a, b, d = split3((-0.5 * LOG2E) * norm)
    out.append(
        jnp.where(row <= 2, 1.0, jnp.where(row == 3, a, jnp.where(row == 4, b, jnp.where(row == 5, d, 0.0))))
    )
    return out


LIST_ROWS = 128
TABLE_ROWS = 2 * LIST_ROWS
LEAF_AT, PTR_AT, COUNT_AT, ROUNDS_AT = 0, 12, 26, 31
GROUP = 16


def plan_kernel(leaves, first, ulist, c0, c1, c2, out, ids):
    slots = ulist.shape[0]
    lane = lax.broadcasted_iota(jnp.int32, (32, 128), 1)
    ids[...] = jnp.full((32, 128), -1, jnp.int32)
    ids[:slots, :leaves] = ulist[...]
    rel = ids[...]
    rel = jnp.where(rel >= 0, rel - first[0], -1)
    counts = [c[0, :1, :].astype(jnp.int32) for c in (c0, c1, c2)]
    nun = [jnp.right_shift(jnp.broadcast_to(c, (32, 128)) + 31, 5) for c in counts]
    low = jnp.where(lane < leaves, nun[0], pltpu.roll(nun[1], leaves, 1))
    from_low = jnp.take_along_axis(low, jnp.clip(rel, 0, 127), axis=1, mode="promise_in_bounds")
    from_high = jnp.take_along_axis(nun[2], jnp.clip(rel - 2 * leaves, 0, 127), axis=1, mode="promise_in_bounds")
    num = jnp.where(rel < 0, 0, jnp.where(rel < 2 * leaves, from_low, from_high))
    before = lax.broadcasted_iota(jnp.int32, (32, 32), 1) < lax.broadcasted_iota(jnp.int32, (32, 32), 0)
    start = 5 + jnp.dot(
        jnp.where(before, 1.0, 0.0).astype(BF), num.astype(F32).astype(BF), preferred_element_type=F32
    ).astype(jnp.int32)
    place = lax.broadcasted_iota(jnp.int32, (LIST_ROWS, 128), 0)
    mine = lax.broadcasted_iota(jnp.int32, (LIST_ROWS, 128), 1)
    unit = jnp.where(place < 4, 12 * leaves + 4 * mine + place, jnp.where(place == 4, 16 * leaves + mine, 17 * leaves))
    for s in range(slots):
        at = place - start[s : s + 1]
        inside = (at >= 0) & (at < num[s : s + 1])
        unit = jnp.where(inside, 4 * rel[s : s + 1] + at, unit)
    out[:LIST_ROWS, :] = unit
    out[LIST_ROWS:TABLE_ROWS, :] = jnp.bitwise_and(unit, -4) + jnp.bitwise_and(place - unit, 3)
    n = jnp.right_shift(start[31:] + num[31:] + 7, 3)
    n = jnp.where(lane[:1] < leaves, n, 0)
    column = jnp.broadcast_to(n.astype(F32), (128, 128)).T
    upto = lax.broadcasted_iota(jnp.int32, (128, 128), 1) <= lax.broadcasted_iota(jnp.int32, (128, 128), 0)
    end = jnp.dot(jnp.where(upto, 1.0, 0.0).astype(BF), column.astype(BF), preferred_element_type=F32)
    begin = (end - column).astype(jnp.int32)
    end = end.astype(jnp.int32)
    total = end[127:]
    out[TABLE_ROWS:, :] = jnp.zeros((32, 128), jnp.int32)
    for r in range(9):
        chunk = 128 * r + mine
        inside = (chunk >= begin) & (chunk < end)
        leaf = jnp.sum(jnp.where(inside, place, 0), axis=0, keepdims=True)
        ptr = jnp.sum(jnp.where(inside, (chunk - begin) * 1024 + place, 0), axis=0, keepdims=True)
        ptr = jnp.where(chunk[:1] < total, ptr, 120 * 128)
        out[TABLE_ROWS + LEAF_AT + r : TABLE_ROWS + LEAF_AT + r + 1, :] = leaf
        out[TABLE_ROWS + PTR_AT + r : TABLE_ROWS + PTR_AT + r + 1, :] = ptr
    for slab in range(3):
        out[TABLE_ROWS + COUNT_AT + slab : TABLE_ROWS + COUNT_AT + slab + 1, :] = counts[slab]
    out[TABLE_ROWS + ROUNDS_AT :, :] = jnp.right_shift(total + GROUP - 1, 4)


def plan_call(first, ulist, points3):
    leaves = ulist.shape[1]
    row = pl.BlockSpec((1, 8, 128), lambda i: (4, 0, 0))
    return pl.pallas_call(
        functools.partial(plan_kernel, leaves),
        grid=(1,),
        out_shape=jax.ShapeDtypeStruct((TABLE_ROWS + 32, 128), jnp.int32),
        in_specs=[pl.BlockSpec(memory_space=pltpu.SMEM), pl.BlockSpec(memory_space=pltpu.VMEM), row, row, row],
        out_specs=pl.BlockSpec(memory_space=pltpu.VMEM),
        scratch_shapes=[pltpu.VMEM((32, 128), jnp.int32)],
        name="plan",
    )(first, ulist, *points3).reshape(-1)


def near_kernel(leaves, plan, p0, p1, p2, d0, d1, d2, surf, down, down_tail, out, f_s, m_s, w_s, e_s, acc):
    lane = lax.broadcasted_iota(jnp.int32, (32, 128), 1)
    maps = 128 * TABLE_ROWS

    def used(slab, j):
        return plan[maps + 128 * (COUNT_AT + slab) + j]

    lane_big = lax.broadcasted_iota(jnp.int32, (128, 128), 1)
    row_big = lax.broadcasted_iota(jnp.int32, (128, 128), 0)
    zero_unit = 4 * (3 * leaves + leaves + leaves // 4)
    shifts = jnp.concatenate(
        [jnp.where(lane_big == (row_big + 32 * k) % 128, 1.0, 0.0).astype(BF) for k in range(1, 4)], axis=1
    )

    def put_features(coords4, base):
        tiles = []
        for coords in coords4:
            tiles += source_tiles(coords)
        tile = jnp.concatenate(tiles, axis=0).astype(BF)
        turned = tile.T
        for i in range(4):
            own = (lane_big >= 32 * i) & (lane_big < 32 * i + 32)
            f_s[pl.ds(base + 4 * i, 4)] = jnp.where(own, turned, jnp.zeros_like(turned)).reshape(4, 32, 128)

    def put_density(tiles, base):
        parts = []
        for i, tile in enumerate(tiles):
            hi, lo = split2(tile)
            parts.append(jnp.concatenate([hi, lo], axis=0))
            m_s[base + 4 * i] = parts[i]
        moved = jnp.dot(jnp.concatenate(parts, axis=0), shifts, preferred_element_type=F32).astype(BF)
        for i in range(4):
            for k in range(1, 4):
                m_s[base + 4 * i + k] = moved[64 * i : 64 * i + 64, 128 * (k - 1) : 128 * k]

    for slab, (p, d) in enumerate(((p0, d0), (p1, d1), (p2, d2))):

        def prep(g, carry, slab=slab, p=p, d=d):
            for half in range(4):
                first = 16 * g + 4 * half
                coords4 = [[p[c, pl.ds(first + i, 1), :] for c in range(3)] for i in range(4)]
                put_features(coords4, 4 * (slab * leaves + first))
                masked = [
                    jnp.where(lane < used(slab, first + i), d[first + i], 0.0) for i in range(4)
                ]
                put_density(masked, 4 * (slab * leaves + first))
            return carry

        lax.fori_loop(0, leaves // 16, prep, 0)

    def prep_surface(count, row0, view):
        def body(g, carry):
            for half in range(4):
                first = 16 * g + 4 * half
                coords4 = [[surf[c, pl.ds(row0 + first + i, 1), :] for c in range(3)] for i in range(4)]
                put_features(coords4, 4 * (3 * leaves + row0 + first))
                put_density([view(first + i) for i in range(4)], 4 * (3 * leaves + row0 + first))
            return carry

        lax.fori_loop(0, count // 16, body, 0)

    prep_surface(leaves, 0, lambda j: down[j])
    prep_surface(leaves // 4, leaves, lambda j: down_tail[j])
    f_s[pl.ds(zero_unit, 4)] = jnp.zeros((4, 32, 128), BF)
    m_s[pl.ds(zero_unit, 4)] = jnp.zeros((4, 64, 128), BF)

    def prep_target(g, carry):
        for i in range(4):
            j = 4 * g + i
            tile = jnp.concatenate(target_tiles([p1[c, pl.ds(j, 1), :] for c in range(3)]), axis=0).astype(BF)
            w_s[j] = jnp.concatenate([tile] * 4, axis=0)
            acc[j] = jnp.zeros((64, 256), F32)
        return carry

    lax.fori_loop(0, leaves // 4, prep_target, 0)

    lane64 = lax.broadcasted_iota(jnp.int32, (64, 128), 1)

    def exponents(i, slot):
        base, l = plan[maps + 128 * PTR_AT + i], plan[maps + 128 * LEAF_AT + i]
        left = jnp.concatenate([f_s[plan[base + 128 * v]] for v in range(4)], axis=0)
        right = jnp.concatenate([f_s[plan[base + 128 * (4 + v)]] for v in range(4)], axis=0)
        w = w_s[l]
        e_s[slot, 0] = jnp.dot(left, w, preferred_element_type=F32)
        e_s[slot, 1] = jnp.dot(right, w, preferred_element_type=F32)

    def weights(base):
        t = [m_s[plan[base + 128 * v]] for v in range(4)]
        return jnp.where(
            lane64 < 64, jnp.where(lane64 < 32, t[0], t[1]), jnp.where(lane64 < 96, t[2], t[3])
        )

    def apply(i, slot):
        base, l = plan[maps + 128 * PTR_AT + i], plan[maps + 128 * LEAF_AT + i]
        m = jnp.concatenate([weights(base + 128 * LIST_ROWS), weights(base + 128 * (LIST_ROWS + 4))], axis=1)
        k = jnp.exp2(e_s[slot].reshape(256, 128))
        hi, lo = split2(k)
        acc[l] += jnp.dot(m, jnp.concatenate([hi, lo], axis=1), preferred_element_type=F32)

    half = 8
    for u in range(half):
        exponents(u, u)

    def body(i, carry):
        at = 2 * half * i
        for u in range(half):
            exponents(at + half + u, half + u)
            apply(at + u, u)
        for u in range(half):
            exponents(at + 2 * half + u, u)
            apply(at + half + u, half + u)
        return carry

    lax.fori_loop(0, plan[maps + 128 * ROUNDS_AT], body, 0)

    def finish(g, carry):
        for i in range(4):
            j = 4 * g + i
            a = acc[j]
            v = (a[:32, :128] + a[:32, 128:]) + (a[32:, :128] + a[32:, 128:])
            out[j] = jnp.where(lane < used(1, j), v, 0.0)
        return carry

    lax.fori_loop(0, leaves // 4, finish, 0)


def near_call(plan, pts, dens, surf, down, down_tail):
    leaves = dens[0].shape[0]
    units = 4 * (3 * leaves + leaves + leaves // 4) + 4
    smem = pl.BlockSpec(memory_space=pltpu.SMEM)
    vmem = pl.BlockSpec(memory_space=pltpu.VMEM)
    return pl.pallas_call(
        functools.partial(near_kernel, leaves),
        out_shape=jax.ShapeDtypeStruct(dens[0].shape, F32),
        in_specs=[smem] + [vmem] * 9,
        out_specs=vmem,
        scratch_shapes=[
            pltpu.VMEM((units, 32, 128), BF),
            pltpu.VMEM((units, 64, 128), BF),
            pltpu.VMEM((leaves, 128, 128), BF),
            pltpu.VMEM((16, 2, 128, 128), F32),
            pltpu.VMEM((leaves, 64, 256), F32),
        ],
        compiler_params=pltpu.CompilerParams(vmem_limit_bytes=60 * 1024 * 1024),
        name="near",
    )(plan, *pts, *dens, surf, down, down_tail)


def dot3(a, b):
    ah, al = split2(a)
    bh, bl = split2(b)
    left = jnp.concatenate([ah, al], axis=0)
    r = jnp.dot(left, bh, preferred_element_type=F32)
    m = a.shape[0]
    return r[:m] + (r[m:] + jnp.dot(ah, bl, preferred_element_type=F32))


def up_kernel(
    pts, dens, surf, sel, up_inv, down_inv, shift_up, shift_down, coarse, table,
    pts_lo, pts_hi, dens_lo, dens_hi, down, down_tail,
    check, node, nodes, near_top, far_top, held, sources, far_sum, picked, leaf_sum, send, recv, table_sem,
):
    leaves, q_width = dens.shape[0], dens.shape[1]
    width = up_inv.shape[0]
    count = lax.axis_size("oct")
    me = lax.axis_index("oct")
    right = lax.rem(me + 1, count)
    left = lax.rem(me + count - 1, count)
    child = lax.rem(me, 8)
    row = me // 8
    rows = count // 8
    mates = [me - child + lax.rem(child + k, 8) for k in range(1, 8)]
    cousins = [lax.rem(row + k, rows) * 8 + child for k in range(1, rows)]

    def fetch(b):
        part = pl.ds(pl.multiple_of(STEP * width * b, 16), STEP * width)
        return pltpu.make_async_copy(table.at[part], held.at[part], table_sem.at[b])

    def fetch_start(b, carry):
        fetch(b).start()
        return carry

    blocks = width // STEP
    lax.fori_loop(0, blocks, fetch_start, 0)
    barrier = pltpu.get_barrier_semaphore()
    for other in [left, right] + mates + cousins:
        pl.semaphore_signal(barrier, inc=1, device_id=(other,), device_id_type=pl.DeviceIdType.MESH)
    pl.semaphore_wait(barrier, 2 + len(mates) + len(cousins))

    def push(src, dst, sem, device):
        copy = pltpu.make_async_remote_copy(
            src_ref=src, dst_ref=dst, send_sem=send.at[sem], recv_sem=recv.at[sem],
            device_id=(device,), device_id_type=pl.DeviceIdType.MESH,
        )
        copy.start()
        return copy

    halo = [
        push(pts, pts_lo, 0, right),
        push(pts, pts_hi, 1, left),
        push(dens, dens_lo, 2, right),
        push(dens, dens_hi, 3, left),
    ]

    lane = lax.broadcasted_iota(jnp.int32, (32, 128), 1).astype(F32)
    lane_big = lax.broadcasted_iota(jnp.int32, (128, 128), 1)

    def leaf_group(g, carry):
        tiles = []
        for i in range(4):
            tiles += source_tiles([pts[c, pl.ds(4 * g + i, 1), :] for c in range(3)])
        turned = jnp.concatenate(tiles, axis=0).astype(BF).T
        for i in range(4):
            j = 4 * g + i
            own = (lane_big >= 32 * i) & (lane_big < 32 * i + 32)
            f = jnp.where(own, turned, jnp.zeros_like(turned))
            w = jnp.concatenate(
                [
                    jnp.concatenate(
                        target_tiles([surf[3 * h + c, pl.ds(j, 1), :] for c in range(3)]), axis=0
                    ).astype(BF)
                    for h in range(2)
                ],
                axis=1,
            )
            k = jnp.exp2(jnp.dot(f, jnp.concatenate([w] * 4, axis=0), preferred_element_type=F32))
            hi, lo = split2(k)
            used = jnp.broadcast_to(pts[3, pl.ds(j, 1), :], (32, 128))
            mh, ml = split2(jnp.where(lane < used, dens[j], 0.0))
            r = jnp.dot(
                jnp.concatenate([mh, ml], axis=0), jnp.concatenate([hi, lo], axis=1), preferred_element_type=F32
            )
            c = 4 * lax.rem(g, 2) + i
            n = g // 2
            check[c, pl.ds(pl.multiple_of(32 * n, 32), 32), :] = (r[:32, :256] + r[:32, 256:]) + (
                r[32:, :256] + r[32:, 256:]
            )
        return carry

    lax.fori_loop(0, leaves // 4, leaf_group, 0)
    node[...] = jnp.zeros_like(node)
    far_sum[...] = jnp.zeros_like(far_sum)

    def merge(half, carry):
        parts = []
        for i in range(4):
            both = dot3(up_inv[...], shift_up[4 * half + i])
            parts.append(dot3(check[4 * half + i][:, :width], both))
        node[...] += (parts[0] + parts[1]) + (parts[2] + parts[3])
        return carry

    lax.fori_loop(0, 2, merge, 0)
    nodes[1, :, :width] = node[...].astype(BF)
    halo.append(push(nodes.at[1], nodes.at[0], 4, right))
    halo.append(push(nodes.at[1], nodes.at[2], 5, left))

    def climb(c, total):
        return total + dot3(node[pl.ds(pl.multiple_of(32 * c, 32), 32), :], shift_up[c])

    top = lax.fori_loop(0, 8, climb, jnp.zeros((q_width, width), F32))
    near_top[0, :, :width] = dot3(top, shift_up[child])
    copies = [push(near_top.at[0], near_top.at[k], 5 + k, mates[k - 1]) for k in range(1, 8)]

    def turn(slab):
        x = nodes[slab].astype(F32)
        for i in range(8):
            rows32 = x[32 * i : 32 * i + 32]
            turned = jnp.concatenate([rows32] * 4, axis=0).T
            sources[slab, :, i, :] = turned[:width]

    turn(1)
    for copy in halo[4:]:
        copy.wait_recv()
    turn(0)
    turn(2)

    def far_block(b, carry):
        fetch(b).wait()
        part = pl.ds(pl.multiple_of(STEP * width * b, 16), STEP * width)
        picked[...] = jnp.dot(held[part, :], sel[...], preferred_element_type=F32)
        far_step(far_sum, picked, lambda k: [sources[h, STEP * b + k] for h in range(3)], width)
        return carry

    lax.fori_loop(0, blocks // 3, far_block, 0)
    for copy in copies:
        copy.wait_recv()
    top1 = near_top[0, :, :width]
    for k in range(1, 8):
        top1 = top1 + near_top[k, :, :width]
    far_top[0, :, :width] = top1
    more = [push(far_top.at[0], far_top.at[k], 12 + k, cousins[k - 1]) for k in range(1, rows)]
    total = dot3(top1, coarse[child])
    lax.fori_loop(blocks // 3, 2 * blocks // 3, far_block, 0)
    for copy in more:
        copy.wait_recv()
    half = row // 8
    own = jnp.zeros((q_width, width), F32)
    other = jnp.zeros((q_width, width), F32)
    for k in range(8):
        src = lax.rem(row + rows - k, rows)
        pair = dot3(jnp.concatenate([far_top[k, :, :width], far_top[k + 8, :, :width]], axis=0), shift_up[lax.rem(src, 8)])
        same = jnp.where(src // 8 == half, 1.0, 0.0)
        a, b = pair[:q_width], pair[q_width:]
        own = own + (same * a + (1.0 - same) * b)
        other = other + ((1.0 - same) * a + same * b)
    top3 = dot3(own, shift_up[half]) + dot3(other, shift_up[1 - half])
    total = total + dot3(own, coarse[lax.rem(row, 8)]) + dot3(top3, coarse[half])
    lax.fori_loop(2 * blocks // 3, blocks, far_block, 0)
    node[...] = far_sum[...].T[:, :width]

    for c in range(8):
        at = slice(32 * c, 32 * c + 32)
        node[at, :] = node[at, :] + dot3(total, shift_down[c])
    leaf_sum[...] = jnp.zeros_like(leaf_sum)

    def descend(half, carry):
        tail = None
        for i in range(4):
            leaf_sum[i, :, :width] = dot3(node[...], dot3(shift_down[4 * half + i], down_inv[...]))
            last = leaf_sum[i, :, 128:]
            last = last if i == 0 else pltpu.roll(last, 32 * i, 1)
            tail = last if tail is None else tail + last
        for n in range(8):
            at = slice(32 * n, 32 * n + 32)
            for i in range(4):
                down[8 * n + 4 * half + i] = leaf_sum[i, at, :128]
            down_tail[2 * n + half] = tail[at]
        return carry

    lax.fori_loop(0, 2, descend, 0)
    for copy in halo[:4]:
        copy.wait_recv()
    for copy in halo + copies + more:
        copy.wait_send()


STEP = 8


def far_step(far_sum, picked, rows_at, width):
    lane = lax.broadcasted_iota(jnp.int32, (32, 128), 1)
    zero = jnp.zeros((32, 128), BF)
    owns = [(lane >= 32 * n) & (lane < 32 * n + 32) for n in range(4)]
    for half in range(2):
        cols = slice(128 * half, 128 * half + 128)
        total = None
        for k in range(0, STEP, 2):
            sums = []
            rows = []
            for e in (k, k + 1):
                s = picked[width * e : width * e + width, cols]
                hi = s.astype(BF).astype(F32)
                sums.append(jnp.concatenate([hi, s - hi], axis=0).astype(BF))
                x = jnp.concatenate(rows_at(e) + [jnp.zeros((8, 128), F32)], axis=0).astype(BF)
                rows += [jnp.where(own, x, zero) for own in owns]
            r = jnp.dot(
                jnp.concatenate(sums, axis=1), jnp.concatenate(rows, axis=0), preferred_element_type=F32
            )
            r = r[:width] + r[width:]
            total = r if total is None else total + r
        far_sum[:width, cols] += total


def up_call(pts, dens, surf, sel, up_inv, down_inv, shift_up, shift_down, coarse, table):
    leaves, q_width, _ = dens.shape
    width = up_inv.shape[0]
    vmem = pl.BlockSpec(memory_space=pltpu.VMEM)
    hbm = pl.BlockSpec(memory_space=pl.ANY)
    like = jax.ShapeDtypeStruct
    rows = 8 * q_width
    return pl.pallas_call(
        up_kernel,
        out_shape=[
            like(pts.shape, F32), like(pts.shape, F32), like(dens.shape, F32), like(dens.shape, F32),
            like((leaves, q_width, 128), F32), like((leaves // 4, q_width, 128), F32),
        ],
        in_specs=[vmem] * 9 + [hbm],
        out_specs=[hbm] * 4 + [vmem] * 2,
        scratch_shapes=[
            pltpu.VMEM((8, rows, 256), F32),
            pltpu.VMEM((rows, width), F32),
            pltpu.VMEM((3, rows, 256), BF),
            pltpu.VMEM((8, q_width, 256), F32),
            pltpu.VMEM((16, q_width, 256), F32),
            pltpu.VMEM(table.shape, BF),
            pltpu.VMEM((3, width, 8, 128), F32),
            pltpu.VMEM((256, rows), F32),
            pltpu.VMEM((STEP * width, 256), F32),
            pltpu.VMEM((4, rows, 256), F32),
            pltpu.SemaphoreType.DMA((28,)),
            pltpu.SemaphoreType.DMA((28,)),
            pltpu.SemaphoreType.DMA((width // STEP,)),
        ],
        compiler_params=pltpu.CompilerParams(
            vmem_limit_bytes=56 * 1024 * 1024, collective_id=0, has_side_effects=True
        ),
        name="upward",
    )(pts, dens, surf, sel, up_inv, down_inv, shift_up, shift_down, coarse, table)


def local(
    points,
    dens,
    surface,
    counts,
    ulist,
    vlist,
    up_inverse,
    down_inverse,
    shift_up,
    shift_down,
    coarse,
    translate,
):
    leaf_count, _, p_width = dens.shape
    eq_width = surface.shape[2]
    node_count = vlist.shape[0]
    index = lax.axis_index("oct")
    used = counts.astype(F32)
    turned_points = jnp.concatenate(
        [
            jnp.transpose(points, (1, 0, 2)),
            jnp.broadcast_to(used[None, :, None], (1, leaf_count, p_width)),
            jnp.broadcast_to(jnp.pad(used, (0, p_width - leaf_count))[None, None, :], (1, leaf_count, p_width)),
        ],
        axis=0,
    )
    turned_surface = jnp.transpose(surface, (1, 0, 2))
    surf_tail = jnp.pad(turned_surface[:, :, 128:], ((0, 0), (0, 0), (0, 160 - eq_width)))
    surf = jnp.concatenate(
        [turned_surface[:, :, :128], jnp.pad(surf_tail, ((0, 0), (0, 0), (0, 96)))], axis=0
    )
    surf_near = jnp.concatenate([turned_surface[:, :, :128], surf_tail.reshape(3, leaf_count // 4, 128)], axis=1)
    rel = jnp.where(vlist >= 0, vlist - (index - 1) * node_count, -1)
    sel = (rel.T[:, :, None] == jnp.arange(32)).astype(BF).reshape(rel.shape[1], 256)
    points_lo, points_hi, dens_lo, dens_hi, leaf_down, down_tail = up_call(
        turned_points, dens, surf, sel, up_inverse, down_inverse, shift_up, shift_down, coarse,
        jnp.transpose(translate, (1, 2, 0)).reshape(eq_width * eq_width, -1),
    )
    points3 = [points_lo, turned_points, points_hi]
    first = ((index - 1) * leaf_count).astype(jnp.int32).reshape(1)
    plan = plan_call(first, jnp.transpose(ulist), points3)
    return near_call(plan, points3, [dens_lo, dens, dens_hi], surf_near, leaf_down, down_tail)


def solution(mesh):
    placed = (
        P("oct", None, None),
        P("oct", None, None),
        P("oct", None, None),
        P("oct"),
        P("oct", None),
        P("oct", None),
        P(),
        P(),
        P(),
        P(),
        P(),
        P(),
    )
    return jax.shard_map(
        local, mesh=mesh, in_specs=placed, out_specs=P("oct", None, None), check_vma=False
    )
```

time: 121 us -> 110 us (0.909); the launches traced: 119 us -> 110 us
  local copies, waits for them, and re-layouts: 6.05 us -> 2.22 us
  other arithmetic: 8.76 us -> 4.99 us
    pallas_call x1, Pallas kernels: 45 us -> 38 us  [near_call(): pl.pallas_call(functools.partial(near_kernel, leaves), out_shape=jax.Shap...]
    pallas_call x1, Pallas kernels: 58.4 us -> 62.2 us  [up_call(): pl.pallas_call(up_kernel, out_shape=[like(pts.shape, F32), like(pts.shape...]
    reduce_sum x6 -> x0, other arithmetic: 2.9 us -> none  [the longest x1 1 us: make_lists(): jnp.sum(jnp.where(inside, 4 * rel[:, :, None] + at - zero_unit, 0), axis=1)]
    pallas_call x0 -> x1, Pallas kernels: none -> 2.5 us  [plan_call(): pl.pallas_call(functools.partial(plan_kernel, leaves), grid=(1,), out_sha...]
    reshape x1, local copies, waits for them, and re-layouts: 1.46 us -> 0.08 us  [local(): surf_tail.reshape(3, leaf_count // 4, 128)]
    select_n x2 -> x0, other arithmetic: 1.25 us -> none  [the longest x1 1.24 us: make_lists(): ptr = jnp.where(chunk < end[-1], ptr, 256 * leaves)]
    concatenate x2 -> x3, other arithmetic: 2.24 us -> 2.93 us  [the longest x1 1.58 us: local(): jnp.concatenate([jnp.transpose(points, (1, 0, 2)), jnp.broadcast_to(used[...]
where the time goes in v4:
time: 110 us
  Pallas kernels  103 us (94%)
  other arithmetic  4.99 us (5%)
  local copies, waits for them, and re-layouts  2.22 us (2%)
    pallas_call x1, Pallas kernels, up_call(): pl.pallas_call(up_kernel, out_shape=[like(pts.shape, F32), like(pts.shape...  62.2 us
    pallas_call x1, Pallas kernels, near_call(): pl.pallas_call(functools.partial(near_kernel, leaves), out_shape=jax.Shap...  38 us
    pallas_call x1, Pallas kernels, plan_call(): pl.pallas_call(functools.partial(plan_kernel, leaves), grid=(1,), out_sha...  2.5 us

profile of v4, /device:TPU:1, one launch (start us, length us, event | category | flops | bytes accessed | tf_op | source)
XLA Modules:
  0.0 109.9 jit_solution(17312878901175192579)
XLA Ops:
  0.0 0.7 convert_element_type.13
  0.7 0.1 eq.23
  0.7 0.7 select_bitcast_fusion
  1.5 0.1 broadcast_in_dim.7
  1.5 1.6 %pad_maximum_fusion.pts.c1.p1 = f32[5,64,128]{2,1,0:T(8,128)} fusion(f32[1,64,128]{2,1,0:T(8,128)S(1)} %broadcast_in_dim.8, f32[1,64,128]{2,1,0:T(8,128)S(1)} %broadcast_in_dim.7, f32[3,64,128]{2,1,0:T(8,128)} %bitcast.16), kind=kLoop, calls=%fused_computation.3 | loop fusion | flops 81920 | bytes 327680 | tf_op jit(solution)/shard_map/concatenate | solution.py:556
  3.1 0.9 slice.9
  4.0 0.9 slice.10
  4.9 0.1 reshape.25
  5.0 0.7 select_maximum_fusion.surf
  5.7 0.7 pad_maximum_fusion.1.surf
  6.4 0.1 copy.14
  6.6 0.7 compare_convert_fusion.sel
  7.2 62.2 %upward.1 = (f32[5,64,128]{2,1,0:T(8,128)}, f32[5,64,128]{2,1,0:T(8,128)}, f32[64,32,128]{2,1,0:T(8,128)}, f32[64,32,128]{2,1,0:T(8,128)}, f32[64,32,128]{2,1,0:T(8,128)}, /*index=5*/f32[16,32,128]{2,1,0:T(8,128)}) custom-call(f32[5,64,128]{2,1,0:T(8,128)} %pad_maximum_fusion.pts.c1.p1, f32[64,32,128]{2,1,0:T(8,128)} %d1.1, ...), custom_call_target="tpu_custom_call" | custom-call | tf_op jit(solution)/shard_map/upward/pallas_call | solution.py:507
  69.5 2.5 %plan.1 = s32[288,128]{1,0:T(8,128)} custom-call(s32[1]{0:T(128)} %bitcast.first, s32[27,64]{1,0:T(8,128)} %bitcast.17, f32[5,64,128]{2,1,0:T(8,128)} %get-tuple-element.11.c0.p0, f32[5,64,128]{2,1,0:T(8,128)} %pad_maximum_fusion.pts.c1.p1, f32[5,64,128]{2,1,0:T(8,128)} %get-tuple-element.12.c2.p2), custom_call_target="tpu_custom_call" | custom-call | tf_op jit(solution)/shard_map/plan/pallas_call | solution.py:126
  72.0 38.0 %near.1 = f32[64,32,128]{2,1,0:T(8,128)} custom-call(s32[36864]{0:T(1024)} %bitcast.13, f32[5,64,128]{2,1,0:T(8,128)} %get-tuple-element.11.c0.p0, f32[5,64,128]{2,1,0:T(8,128)} %pad_maximum_fusion.pts.c1.p1, f32[5,64,128]{2,1,0:T(8,128)} %get-tuple-element.12.c2.p2, f32[64,32,128]{2,1,0:T(8,128)} %get-tuple-element.13.d0, f32[64,32,128]{2,1,0:T(8,128)} %d1.1, ...), custom_call_target="tpu_custom_call" | custom-call | tf_op jit(solution)/shard_map/near/pallas_call | solution.py:268
  (5 shorter events, 0.0 us)

commit v5 on v4

--- a/solution.py
+++ b/solution.py
@@ -72,14 +72,14 @@
 GROUP = 16
 
 
-def plan_kernel(leaves, first, ulist, c0, c1, c2, out, ids):
+def plan_kernel(leaves, first, ulist, rows, out, ids):
     slots = ulist.shape[0]
     lane = lax.broadcasted_iota(jnp.int32, (32, 128), 1)
     ids[...] = jnp.full((32, 128), -1, jnp.int32)
     ids[:slots, :leaves] = ulist[...]
     rel = ids[...]
     rel = jnp.where(rel >= 0, rel - first[0], -1)
-    counts = [c[0, :1, :].astype(jnp.int32) for c in (c0, c1, c2)]
+    counts = [rows[slab, :1, :] for slab in range(3)]
     nun = [jnp.right_shift(jnp.broadcast_to(c, (32, 128)) + 31, 5) for c in counts]
     low = jnp.where(lane < leaves, nun[0], pltpu.roll(nun[1], leaves, 1))
     from_low = jnp.take_along_axis(low, jnp.clip(rel, 0, 127), axis=1, mode="promise_in_bounds")
@@ -120,18 +120,17 @@
     out[TABLE_ROWS + ROUNDS_AT :, :] = jnp.right_shift(total + GROUP - 1, 4)
 
 
-def plan_call(first, ulist, points3):
+def plan_call(first, ulist, rows):
     leaves = ulist.shape[1]
-    row = pl.BlockSpec((1, 8, 128), lambda i: (4, 0, 0))
+    vmem = pl.BlockSpec(memory_space=pltpu.VMEM)
     return pl.pallas_call(
         functools.partial(plan_kernel, leaves),
-        grid=(1,),
         out_shape=jax.ShapeDtypeStruct((TABLE_ROWS + 32, 128), jnp.int32),
-        in_specs=[pl.BlockSpec(memory_space=pltpu.SMEM), pl.BlockSpec(memory_space=pltpu.VMEM), row, row, row],
-        out_specs=pl.BlockSpec(memory_space=pltpu.VMEM),
+        in_specs=[pl.BlockSpec(memory_space=pltpu.SMEM), vmem, vmem],
+        out_specs=vmem,
         scratch_shapes=[pltpu.VMEM((32, 128), jnp.int32)],
         name="plan",
-    )(first, ulist, *points3).reshape(-1)
+    )(first, ulist, rows).reshape(-1)
 
 
 def near_kernel(leaves, plan, p0, p1, p2, d0, d1, d2, surf, down, down_tail, out, f_s, m_s, w_s, e_s, acc):
@@ -292,9 +291,9 @@
 
 
 def up_kernel(
-    pts, dens, surf, sel, up_inv, down_inv, shift_up, shift_down, coarse, table,
-    pts_lo, pts_hi, dens_lo, dens_hi, down, down_tail,
-    check, node, nodes, near_top, far_top, held, sources, far_sum, picked, leaf_sum, send, recv, table_sem,
+    counts, pts, dens, surf, count_row, vlist, up_inv, down_inv, shift_up, shift_down, coarse, table,
+    pts_lo, pts_hi, dens_lo, dens_hi, count_rows, surf_near, down, down_tail,
+    check, node, nodes, near_top, far_top, held, sources, far_sum, leaf_sum, surf_pad, sel_turned, picker, send, recv, table_sem,
 ):
     leaves, q_width = dens.shape[0], dens.shape[1]
     width = up_inv.shape[0]
@@ -309,7 +308,7 @@
     cousins = [lax.rem(row + k, rows) * 8 + child for k in range(1, rows)]
 
     def fetch(b):
-        part = pl.ds(pl.multiple_of(STEP * width * b, 16), STEP * width)
+        part = pl.ds(pl.multiple_of(STEP * b, STEP), STEP)
         return pltpu.make_async_copy(table.at[part], held.at[part], table_sem.at[b])
 
     def fetch_start(b, carry):
@@ -331,49 +330,74 @@
         copy.start()
         return copy
 
+    count_rows[1] = jnp.zeros((8, 128), jnp.int32)
+    count_rows[1, :1, :leaves] = count_row[...]
     halo = [
+        push(count_rows.at[1], count_rows.at[0], 28, right),
+        push(count_rows.at[1], count_rows.at[2], 29, left),
         push(pts, pts_lo, 0, right),
         push(pts, pts_hi, 1, left),
         push(dens, dens_lo, 2, right),
         push(dens, dens_hi, 3, left),
     ]
 
-    lane = lax.broadcasted_iota(jnp.int32, (32, 128), 1).astype(F32)
+    surf_pad[...] = jnp.zeros_like(surf_pad)
+    surf_pad[:, :, : width - 128] = surf[:, :, 128:]
+    surf_near[:, :leaves, :] = surf[:, :, :128]
+    for c in range(3):
+        packed = None
+        for i in range(4):
+            last = surf_pad[c, pl.ds(i, leaves // 4, stride=4), :]
+            last = last if i == 0 else pltpu.roll(last, 32 * i, 1)
+            packed = last if packed is None else packed + last
+        surf_near[c, leaves:, :] = packed
+    rel = vlist[...]
+    rel = jnp.where(rel >= 0, rel - (me - 1) * 8, -1)
+    types = rel.shape[1]
+    sel_turned[...] = jnp.zeros_like(sel_turned)
+    for n in range(8):
+        same = jnp.broadcast_to(rel[n : n + 1], (32, types)) == rows8((32, types))
+        sel_turned[32 * n : 32 * n + 32, :types] = jnp.where(same, 1.0, 0.0)
+    picker[...] = sel_turned[...].T[:types].astype(BF)
+    lane = lax.broadcasted_iota(jnp.int32, (32, 128), 1)
     lane_big = lax.broadcasted_iota(jnp.int32, (128, 128), 1)
 
     def leaf_group(g, carry):
-        tiles = []
-        for i in range(4):
-            tiles += source_tiles([pts[c, pl.ds(4 * g + i, 1), :] for c in range(3)])
-        turned = jnp.concatenate(tiles, axis=0).astype(BF).T
-        for i in range(4):
-            j = 4 * g + i
-            own = (lane_big >= 32 * i) & (lane_big < 32 * i + 32)
-            f = jnp.where(own, turned, jnp.zeros_like(turned))
-            w = jnp.concatenate(
-                [
-                    jnp.concatenate(
-                        target_tiles([surf[3 * h + c, pl.ds(j, 1), :] for c in range(3)]), axis=0
-                    ).astype(BF)
-                    for h in range(2)
-                ],
-                axis=1,
-            )
-            k = jnp.exp2(jnp.dot(f, jnp.concatenate([w] * 4, axis=0), preferred_element_type=F32))
-            hi, lo = split2(k)
-            used = jnp.broadcast_to(pts[3, pl.ds(j, 1), :], (32, 128))
-            mh, ml = split2(jnp.where(lane < used, dens[j], 0.0))
-            r = jnp.dot(
-                jnp.concatenate([mh, ml], axis=0), jnp.concatenate([hi, lo], axis=1), preferred_element_type=F32
-            )
-            c = 4 * lax.rem(g, 2) + i
-            n = g // 2
-            check[c, pl.ds(pl.multiple_of(32 * n, 32), 32), :] = (r[:32, :256] + r[:32, 256:]) + (
-                r[32:, :256] + r[32:, 256:]
-            )
-        return carry
-
-    lax.fori_loop(0, leaves // 4, leaf_group, 0)
+        at = pl.ds(pl.multiple_of(8 * g, 8), 8)
+        points8 = [pts[c, at, :] for c in range(3)]
+        main8 = [surf_near[c, at, :] for c in range(3)]
+        tail8 = [surf_pad[c, at, :] for c in range(3)]
+        for half in range(2):
+            tiles = []
+            for i in range(4):
+                r = 4 * half + i
+                tiles += source_tiles([x[r : r + 1] for x in points8])
+            turned = jnp.concatenate(tiles, axis=0).astype(BF).T
+            for i in range(4):
+                r = 4 * half + i
+                own = (lane_big >= 32 * i) & (lane_big < 32 * i + 32)
+                f = jnp.where(own, turned, jnp.zeros_like(turned))
+                w = jnp.concatenate(
+                    [
+                        jnp.concatenate(target_tiles([x[r : r + 1] for x in part]), axis=0).astype(BF)
+                        for part in (main8, tail8)
+                    ],
+                    axis=1,
+                )
+                k = jnp.exp2(jnp.dot(f, jnp.concatenate([w] * 4, axis=0), preferred_element_type=F32))
+                hi, lo = split2(k)
+                mh, ml = split2(jnp.where(lane < counts[8 * g + r], dens[8 * g + r], 0.0))
+                p = jnp.dot(
+                    jnp.concatenate([mh, ml], axis=0),
+                    jnp.concatenate([hi, lo], axis=1),
+                    preferred_element_type=F32,
+                )
+                check[r, pl.ds(pl.multiple_of(32 * g, 32), 32), :] = (p[:32, :256] + p[:32, 256:]) + (
+                    p[32:, :256] + p[32:, 256:]
+                )
+        return carry
+
+    lax.fori_loop(0, leaves // 8, leaf_group, 0)
     node[...] = jnp.zeros_like(node)
     far_sum[...] = jnp.zeros_like(far_sum)
 
@@ -405,16 +429,15 @@
             sources[slab, :, i, :] = turned[:width]
 
     turn(1)
-    for copy in halo[4:]:
+    for copy in halo[6:]:
         copy.wait_recv()
     turn(0)
     turn(2)
+    picks = picker[...]
 
     def far_block(b, carry):
         fetch(b).wait()
-        part = pl.ds(pl.multiple_of(STEP * width * b, 16), STEP * width)
-        picked[...] = jnp.dot(held[part, :], sel[...], preferred_element_type=F32)
-        far_step(far_sum, picked, lambda k: [sources[h, STEP * b + k] for h in range(3)], width)
+        far_sum[:width, :] += far_step(lambda k: held[STEP * b + k], picks, lambda k: [sources[h, STEP * b + k] for h in range(3)], width)
         return carry
 
     lax.fori_loop(0, blocks // 3, far_block, 0)
@@ -464,7 +487,7 @@
         return carry
 
     lax.fori_loop(0, 2, descend, 0)
-    for copy in halo[:4]:
+    for copy in halo[:6]:
         copy.wait_recv()
     for copy in halo + copies + more:
         copy.wait_send()
@@ -473,31 +496,31 @@
 STEP = 8
 
 
-def far_step(far_sum, picked, rows_at, width):
+def far_step(table_at, picks, rows_at, width):
     lane = lax.broadcasted_iota(jnp.int32, (32, 128), 1)
     zero = jnp.zeros((32, 128), BF)
-    owns = [(lane >= 32 * n) & (lane < 32 * n + 32) for n in range(4)]
-    for half in range(2):
-        cols = slice(128 * half, 128 * half + 128)
-        total = None
-        for k in range(0, STEP, 2):
-            sums = []
-            rows = []
-            for e in (k, k + 1):
-                s = picked[width * e : width * e + width, cols]
-                hi = s.astype(BF).astype(F32)
-                sums.append(jnp.concatenate([hi, s - hi], axis=0).astype(BF))
-                x = jnp.concatenate(rows_at(e) + [jnp.zeros((8, 128), F32)], axis=0).astype(BF)
-                rows += [jnp.where(own, x, zero) for own in owns]
-            r = jnp.dot(
-                jnp.concatenate(sums, axis=1), jnp.concatenate(rows, axis=0), preferred_element_type=F32
-            )
-            r = r[:width] + r[width:]
-            total = r if total is None else total + r
-        far_sum[:width, cols] += total
-
-
-def up_call(pts, dens, surf, sel, up_inv, down_inv, shift_up, shift_down, coarse, table):
+    total = None
+    for k in range(0, STEP, 2):
+        sums = []
+        rows = []
+        for e in (k, k + 1):
+            s = jnp.dot(table_at(e), picks, preferred_element_type=F32)
+            hi, lo = split2(s)
+            sums.append(jnp.concatenate([hi, lo], axis=0))
+            x = jnp.concatenate(rows_at(e) + [jnp.zeros((8, 128), F32)], axis=0).astype(BF)
+            for n in range(8):
+                own = (lane >= 32 * (n % 4)) & (lane < 32 * (n % 4) + 32)
+                part = jnp.where(own, x, zero)
+                rows.append(jnp.concatenate([part, zero] if n < 4 else [zero, part], axis=1))
+        r = jnp.dot(
+            jnp.concatenate(sums, axis=1), jnp.concatenate(rows, axis=0), preferred_element_type=F32
+        )
+        r = r[:width] + r[width:]
+        total = r if total is None else total + r
+    return total
+
+
+def up_call(counts, pts, dens, surf, count_row, vlist, up_inv, down_inv, shift_up, shift_down, coarse, table):
     leaves, q_width, _ = dens.shape
     width = up_inv.shape[0]
     vmem = pl.BlockSpec(memory_space=pltpu.VMEM)
@@ -508,10 +531,11 @@
         up_kernel,
         out_shape=[
             like(pts.shape, F32), like(pts.shape, F32), like(dens.shape, F32), like(dens.shape, F32),
+            like((3, 8, 128), jnp.int32), like((3, leaves + leaves // 4, 128), F32),
             like((leaves, q_width, 128), F32), like((leaves // 4, q_width, 128), F32),
         ],
-        in_specs=[vmem] * 9 + [hbm],
-        out_specs=[hbm] * 4 + [vmem] * 2,
+        in_specs=[pl.BlockSpec(memory_space=pltpu.SMEM)] + [vmem] * 10 + [hbm],
+        out_specs=[hbm] * 4 + [vmem] * 4,
         scratch_shapes=[
             pltpu.VMEM((8, rows, 256), F32),
             pltpu.VMEM((rows, width), F32),
@@ -521,17 +545,19 @@
             pltpu.VMEM(table.shape, BF),
             pltpu.VMEM((3, width, 8, 128), F32),
             pltpu.VMEM((256, rows), F32),
-            pltpu.VMEM((STEP * width, 256), F32),
             pltpu.VMEM((4, rows, 256), F32),
-            pltpu.SemaphoreType.DMA((28,)),
-            pltpu.SemaphoreType.DMA((28,)),
+            pltpu.VMEM((3, leaves, 128), F32),
+            pltpu.VMEM((256, 384), F32),
+            pltpu.VMEM((vlist.shape[1], 256), BF),
+            pltpu.SemaphoreType.DMA((30,)),
+            pltpu.SemaphoreType.DMA((30,)),
             pltpu.SemaphoreType.DMA((width // STEP,)),
         ],
         compiler_params=pltpu.CompilerParams(
             vmem_limit_bytes=56 * 1024 * 1024, collective_id=0, has_side_effects=True
         ),
         name="upward",
-    )(pts, dens, surf, sel, up_inv, down_inv, shift_up, shift_down, coarse, table)
+    )(counts, pts, dens, surf, count_row, vlist, up_inv, down_inv, shift_up, shift_down, coarse, table)
 
 
 def local(
@@ -548,34 +574,16 @@
     coarse,
     translate,
 ):
-    leaf_count, _, p_width = dens.shape
-    eq_width = surface.shape[2]
-    node_count = vlist.shape[0]
+    leaf_count = dens.shape[0]
     index = lax.axis_index("oct")
-    used = counts.astype(F32)
-    turned_points = jnp.concatenate(
-        [
-            jnp.transpose(points, (1, 0, 2)),
-            jnp.broadcast_to(used[None, :, None], (1, leaf_count, p_width)),
-            jnp.broadcast_to(jnp.pad(used, (0, p_width - leaf_count))[None, None, :], (1, leaf_count, p_width)),
-        ],
-        axis=0,
-    )
-    turned_surface = jnp.transpose(surface, (1, 0, 2))
-    surf_tail = jnp.pad(turned_surface[:, :, 128:], ((0, 0), (0, 0), (0, 160 - eq_width)))
-    surf = jnp.concatenate(
-        [turned_surface[:, :, :128], jnp.pad(surf_tail, ((0, 0), (0, 0), (0, 96)))], axis=0
-    )
-    surf_near = jnp.concatenate([turned_surface[:, :, :128], surf_tail.reshape(3, leaf_count // 4, 128)], axis=1)
-    rel = jnp.where(vlist >= 0, vlist - (index - 1) * node_count, -1)
-    sel = (rel.T[:, :, None] == jnp.arange(32)).astype(BF).reshape(rel.shape[1], 256)
-    points_lo, points_hi, dens_lo, dens_hi, leaf_down, down_tail = up_call(
-        turned_points, dens, surf, sel, up_inverse, down_inverse, shift_up, shift_down, coarse,
-        jnp.transpose(translate, (1, 2, 0)).reshape(eq_width * eq_width, -1),
+    turned_points = jnp.transpose(points, (1, 0, 2))
+    points_lo, points_hi, dens_lo, dens_hi, count_rows, surf_near, leaf_down, down_tail = up_call(
+        counts, turned_points, dens, jnp.transpose(surface, (1, 0, 2)), counts.reshape(1, leaf_count), vlist,
+        up_inverse, down_inverse, shift_up, shift_down, coarse, jnp.transpose(translate, (1, 2, 0)),
     )
     points3 = [points_lo, turned_points, points_hi]
     first = ((index - 1) * leaf_count).astype(jnp.int32).reshape(1)
-    plan = plan_call(first, jnp.transpose(ulist), points3)
+    plan = plan_call(first, jnp.transpose(ulist), count_rows)
     return near_call(plan, points3, [dens_lo, dens, dens_hi], surf_near, leaf_down, down_tail)
 
 

time: 110 us -> 95.2 us (0.87)
  Pallas kernels: 103 us -> 94.2 us
  other arithmetic: 4.99 us -> 0 us
  local copies, waits for them, and re-layouts: 2.22 us -> 0 us
    pallas_call x1, Pallas kernels: 62.2 us -> 55.3 us  [up_call(): pl.pallas_call(up_kernel, out_shape=[like(pts.shape, F32), like(pts.shape...]
    concatenate x3 -> x0, other arithmetic: 2.93 us -> none  [the longest x1 1.58 us: local(): jnp.concatenate([jnp.transpose(points, (1, 0, 2)), jnp.broadcast_to(used[...]
    slice x2 -> x0, local copies, waits for them, and re-layouts: 1.8 us -> none  [the longest x1 0.9 us: local(): turned_surface[:, :, :128]]
    pallas_call x1, Pallas kernels: 38 us -> 36.4 us  [near_call(): pl.pallas_call(functools.partial(near_kernel, leaves), out_shape=jax.Shap...]
    convert_element_type x2 -> x0, other arithmetic: 1.35 us -> none  [the longest x1 0.69 us: local(): (rel.T[:, :, None] == jnp.arange(32)).astype(BF).reshape(rel.shape[1], 256)]
where the time goes in v5:
time: 95.2 us; the launch traced here: 94.2 us
  Pallas kernels  94.2 us (99%)
    pallas_call x1, Pallas kernels, up_call(): pl.pallas_call(up_kernel, out_shape=[like(pts.shape, F32), like(pts.shape...  55.3 us
    pallas_call x1, Pallas kernels, near_call(): pl.pallas_call(functools.partial(near_kernel, leaves), out_shape=jax.Shap...  36.4 us
    pallas_call x1, Pallas kernels, plan_call(): pl.pallas_call(functools.partial(plan_kernel, leaves), out_shape=jax.Shap...  2.5 us

profile of v5, /device:TPU:1, one launch (start us, length us, event | category | flops | bytes accessed | tf_op | source)
XLA Modules:
  0.0 94.2 jit_solution(10778616615220686321)
XLA Ops:
  0.0 55.3 %upward.1 = (f32[3,64,128]{2,1,0:T(8,128)}, f32[3,64,128]{2,1,0:T(8,128)}, f32[64,32,128]{2,1,0:T(8,128)}, f32[64,32,128]{2,1,0:T(8,128)}, s32[3,8,128]{2,1,0:T(...) custom-call(s32[64]{0:T(128)} %counts.1, f32[3,64,128]{2,1,0:T(8,128)} %bitcast.9, ...), custom_call_target="tpu_custom_call" | custom-call | tf_op jit(solution)/shard_map/upward/pallas_call | solution.py:530
  55.3 2.5 %plan.1 = s32[288,128]{1,0:T(8,128)} custom-call(s32[1]{0:T(128)} %bitcast.first, s32[27,64]{1,0:T(8,128)} %bitcast.12, s32[3,8,128]{2,1,0:T(8,128)} %get-tuple-element.13.rows), custom_call_target="tpu_custom_call" | custom-call | tf_op jit(solution)/shard_map/plan/pallas_call | solution.py:126
  57.8 36.4 %near.1 = f32[64,32,128]{2,1,0:T(8,128)} custom-call(s32[36864]{0:T(1024)} %bitcast.8, f32[3,64,128]{2,1,0:T(8,128)} %get-tuple-element.14.p0, f32[3,64,128]{2,1,0:T(8,128)} %bitcast.10, f32[3,64,128]{2,1,0:T(8,128)} %get-tuple-element.15.p2, f32[64,32,128]{2,1,0:T(8,128)} %get-tuple-element.16.d0, f32[64,32,128]{2,1,0:T(8,128)} %d1.1, ...), custom_call_target="tpu_custom_call" | custom-call | tf_op jit(solution)/shard_map/near/pallas_call | solution.py:267

commit v6 on v5

--- a/solution.py
+++ b/solution.py
@@ -69,7 +69,7 @@
 LIST_ROWS = 128
 TABLE_ROWS = 2 * LIST_ROWS
 LEAF_AT, PTR_AT, COUNT_AT, ROUNDS_AT = 0, 12, 26, 31
-GROUP = 16
+GROUP = 32
 
 
 def plan_kernel(leaves, first, ulist, rows, out, ids):
@@ -117,7 +117,7 @@
         out[TABLE_ROWS + PTR_AT + r : TABLE_ROWS + PTR_AT + r + 1, :] = ptr
     for slab in range(3):
         out[TABLE_ROWS + COUNT_AT + slab : TABLE_ROWS + COUNT_AT + slab + 1, :] = counts[slab]
-    out[TABLE_ROWS + ROUNDS_AT :, :] = jnp.right_shift(total + GROUP - 1, 4)
+    out[TABLE_ROWS + ROUNDS_AT :, :] = jnp.right_shift(total + GROUP - 1, 5)
 
 
 def plan_call(first, ulist, rows):
@@ -232,7 +232,7 @@
         hi, lo = split2(k)
         acc[l] += jnp.dot(m, jnp.concatenate([hi, lo], axis=1), preferred_element_type=F32)
 
-    half = 8
+    half = 16
     for u in range(half):
         exponents(u, u)
 
@@ -273,7 +273,7 @@
             pltpu.VMEM((units, 32, 128), BF),
             pltpu.VMEM((units, 64, 128), BF),
             pltpu.VMEM((leaves, 128, 128), BF),
-            pltpu.VMEM((16, 2, 128, 128), F32),
+            pltpu.VMEM((32, 2, 128, 128), F32),
             pltpu.VMEM((leaves, 64, 256), F32),
         ],
         compiler_params=pltpu.CompilerParams(vmem_limit_bytes=60 * 1024 * 1024),
@@ -337,8 +337,6 @@
         push(count_rows.at[1], count_rows.at[2], 29, left),
         push(pts, pts_lo, 0, right),
         push(pts, pts_hi, 1, left),
-        push(dens, dens_lo, 2, right),
-        push(dens, dens_hi, 3, left),
     ]
 
     surf_pad[...] = jnp.zeros_like(surf_pad)
@@ -420,6 +418,7 @@
     top = lax.fori_loop(0, 8, climb, jnp.zeros((q_width, width), F32))
     near_top[0, :, :width] = dot3(top, shift_up[child])
     copies = [push(near_top.at[0], near_top.at[k], 5 + k, mates[k - 1]) for k in range(1, 8)]
+    late = [push(dens, dens_lo, 2, right), push(dens, dens_hi, 3, left)]
 
     def turn(slab):
         x = nodes[slab].astype(F32)
@@ -429,7 +428,7 @@
             sources[slab, :, i, :] = turned[:width]
 
     turn(1)
-    for copy in halo[6:]:
+    for copy in halo[4:]:
         copy.wait_recv()
     turn(0)
     turn(2)
@@ -440,7 +439,7 @@
         far_sum[:width, :] += far_step(lambda k: held[STEP * b + k], picks, lambda k: [sources[h, STEP * b + k] for h in range(3)], width)
         return carry
 
-    lax.fori_loop(0, blocks // 3, far_block, 0)
+    lax.fori_loop(0, blocks // 3 + 1, far_block, 0)
     for copy in copies:
         copy.wait_recv()
     top1 = near_top[0, :, :width]
@@ -449,7 +448,7 @@
     far_top[0, :, :width] = top1
     more = [push(far_top.at[0], far_top.at[k], 12 + k, cousins[k - 1]) for k in range(1, rows)]
     total = dot3(top1, coarse[child])
-    lax.fori_loop(blocks // 3, 2 * blocks // 3, far_block, 0)
+    lax.fori_loop(blocks // 3 + 1, blocks - 3, far_block, 0)
     for copy in more:
         copy.wait_recv()
     half = row // 8
@@ -464,7 +463,7 @@
         other = other + ((1.0 - same) * a + same * b)
     top3 = dot3(own, shift_up[half]) + dot3(other, shift_up[1 - half])
     total = total + dot3(own, coarse[lax.rem(row, 8)]) + dot3(top3, coarse[half])
-    lax.fori_loop(2 * blocks // 3, blocks, far_block, 0)
+    lax.fori_loop(blocks - 3, blocks, far_block, 0)
     node[...] = far_sum[...].T[:, :width]
 
     for c in range(8):
@@ -487,9 +486,9 @@
         return carry
 
     lax.fori_loop(0, 2, descend, 0)
-    for copy in halo[:6]:
+    for copy in halo[:4] + late:
         copy.wait_recv()
-    for copy in halo + copies + more:
+    for copy in halo + late + copies + more:
         copy.wait_send()
 
 

time: 95.2 us -> 91.2 us (0.958)
  Pallas kernels: 94.2 us -> 90.9 us
    pallas_call x1, Pallas kernels: 55.3 us -> 53.2 us  [up_call(): pl.pallas_call(up_kernel, out_shape=[like(pts.shape, F32), like(pts.shape...]
    pallas_call x1, Pallas kernels: 36.4 us -> 35.2 us  [near_call(): pl.pallas_call(functools.partial(near_kernel, leaves), out_shape=jax.Shap...]
where the time goes in v6:
time: 91.2 us; the launch traced here: 90.9 us
  Pallas kernels  90.9 us (100%)
    pallas_call x1, Pallas kernels, up_call(): pl.pallas_call(up_kernel, out_shape=[like(pts.shape, F32), like(pts.shape...  53.2 us
    pallas_call x1, Pallas kernels, near_call(): pl.pallas_call(functools.partial(near_kernel, leaves), out_shape=jax.Shap...  35.2 us
    pallas_call x1, Pallas kernels, plan_call(): pl.pallas_call(functools.partial(plan_kernel, leaves), out_shape=jax.Shap...  2.5 us

profile of v6, /device:TPU:1, one launch (start us, length us, event | category | flops | bytes accessed | tf_op | source)
XLA Modules:
  0.0 90.9 jit_solution(7238148620867269893)
XLA Ops:
  0.0 53.2 %upward.1 = (f32[3,64,128]{2,1,0:T(8,128)}, f32[3,64,128]{2,1,0:T(8,128)}, f32[64,32,128]{2,1,0:T(8,128)}, f32[64,32,128]{2,1,0:T(8,128)}, s32[3,8,128]{2,1,0:T(...) custom-call(s32[64]{0:T(128)} %counts.1, f32[3,64,128]{2,1,0:T(8,128)} %bitcast.9, ...), custom_call_target="tpu_custom_call" | custom-call | tf_op jit(solution)/shard_map/upward/pallas_call | solution.py:529
  53.2 2.5 %plan.1 = s32[288,128]{1,0:T(8,128)} custom-call(s32[1]{0:T(128)} %bitcast.first, s32[27,64]{1,0:T(8,128)} %bitcast.12, s32[3,8,128]{2,1,0:T(8,128)} %get-tuple-element.13.rows), custom_call_target="tpu_custom_call" | custom-call | tf_op jit(solution)/shard_map/plan/pallas_call | solution.py:126
  55.7 35.2 %near.1 = f32[64,32,128]{2,1,0:T(8,128)} custom-call(s32[36864]{0:T(1024)} %bitcast.8, f32[3,64,128]{2,1,0:T(8,128)} %get-tuple-element.14.p0, f32[3,64,128]{2,1,0:T(8,128)} %bitcast.10, f32[3,64,128]{2,1,0:T(8,128)} %get-tuple-element.15.p2, f32[64,32,128]{2,1,0:T(8,128)} %get-tuple-element.16.d0, f32[64,32,128]{2,1,0:T(8,128)} %d1.1, ...), custom_call_target="tpu_custom_call" | custom-call | tf_op jit(solution)/shard_map/near/pallas_call | solution.py:267

commit v7 on v6

--- a/solution.py
+++ b/solution.py
@@ -360,7 +360,7 @@
     lane = lax.broadcasted_iota(jnp.int32, (32, 128), 1)
     lane_big = lax.broadcasted_iota(jnp.int32, (128, 128), 1)
 
-    def leaf_group(g, carry):
+    def leaf_node(g):
         at = pl.ds(pl.multiple_of(8 * g, 8), 8)
         points8 = [pts[c, at, :] for c in range(3)]
         main8 = [surf_near[c, at, :] for c in range(3)]
@@ -393,9 +393,13 @@
                 check[r, pl.ds(pl.multiple_of(32 * g, 32), 32), :] = (p[:32, :256] + p[:32, 256:]) + (
                     p[32:, :256] + p[32:, 256:]
                 )
-        return carry
-
-    lax.fori_loop(0, leaves // 8, leaf_group, 0)
+
+    def leaf_group(g, carry):
+        leaf_node(2 * g)
+        leaf_node(2 * g + 1)
+        return carry
+
+    lax.fori_loop(0, leaves // 16, leaf_group, 0)
     node[...] = jnp.zeros_like(node)
     far_sum[...] = jnp.zeros_like(far_sum)
 
@@ -418,7 +422,6 @@
     top = lax.fori_loop(0, 8, climb, jnp.zeros((q_width, width), F32))
     near_top[0, :, :width] = dot3(top, shift_up[child])
     copies = [push(near_top.at[0], near_top.at[k], 5 + k, mates[k - 1]) for k in range(1, 8)]
-    late = [push(dens, dens_lo, 2, right), push(dens, dens_hi, 3, left)]
 
     def turn(slab):
         x = nodes[slab].astype(F32)
@@ -434,12 +437,16 @@
     turn(2)
     picks = picker[...]
 
-    def far_block(b, carry):
-        fetch(b).wait()
-        far_sum[:width, :] += far_step(lambda k: held[STEP * b + k], picks, lambda k: [sources[h, STEP * b + k] for h in range(3)], width)
-        return carry
-
-    lax.fori_loop(0, blocks // 3 + 1, far_block, 0)
+    def far_part(b):
+        return far_step(lambda k: held[STEP * b + k], picks, lambda k: [sources[h, STEP * b + k] for h in range(3)], width)
+
+    def far_pair(b, carry):
+        fetch(2 * b).wait()
+        fetch(2 * b + 1).wait()
+        far_sum[:width, :] += far_part(2 * b) + far_part(2 * b + 1)
+        return carry
+
+    lax.fori_loop(0, 2, far_pair, 0)
     for copy in copies:
         copy.wait_recv()
     top1 = near_top[0, :, :width]
@@ -447,8 +454,9 @@
         top1 = top1 + near_top[k, :, :width]
     far_top[0, :, :width] = top1
     more = [push(far_top.at[0], far_top.at[k], 12 + k, cousins[k - 1]) for k in range(1, rows)]
+    late = [push(dens, dens_lo, 2, right), push(dens, dens_hi, 3, left)]
     total = dot3(top1, coarse[child])
-    lax.fori_loop(blocks // 3 + 1, blocks - 3, far_block, 0)
+    lax.fori_loop(2, blocks // 2, far_pair, 0)
     for copy in more:
         copy.wait_recv()
     half = row // 8
@@ -463,7 +471,9 @@
         other = other + ((1.0 - same) * a + same * b)
     top3 = dot3(own, shift_up[half]) + dot3(other, shift_up[1 - half])
     total = total + dot3(own, coarse[lax.rem(row, 8)]) + dot3(top3, coarse[half])
-    lax.fori_loop(blocks - 3, blocks, far_block, 0)
+    for b in range(2 * (blocks // 2), blocks):
+        fetch(b).wait()
+        far_sum[:width, :] += far_part(b)
     node[...] = far_sum[...].T[:, :width]
 
     for c in range(8):

time: 91.2 us -> 90.3 us (level)
    pallas_call x1, Pallas kernels: 53.2 us -> 52.3 us  [up_call(): pl.pallas_call(up_kernel, out_shape=[like(pts.shape, F32), like(pts.shape...]
where the time goes in v7:
time: 90.3 us; the launch traced here: 90 us
  Pallas kernels  90 us (100%)
    pallas_call x1, Pallas kernels, up_call(): pl.pallas_call(up_kernel, out_shape=[like(pts.shape, F32), like(pts.shape...  52.3 us
    pallas_call x1, Pallas kernels, near_call(): pl.pallas_call(functools.partial(near_kernel, leaves), out_shape=jax.Shap...  35.3 us
    pallas_call x1, Pallas kernels, plan_call(): pl.pallas_call(functools.partial(plan_kernel, leaves), out_shape=jax.Shap...  2.5 us

profile of v7, /device:TPU:1, one launch (start us, length us, event | category | flops | bytes accessed | tf_op | source)
XLA Modules:
  0.0 90.0 jit_solution(1319554651838428033)
XLA Ops:
  0.0 52.3 %upward.1 = (f32[3,64,128]{2,1,0:T(8,128)}, f32[3,64,128]{2,1,0:T(8,128)}, f32[64,32,128]{2,1,0:T(8,128)}, f32[64,32,128]{2,1,0:T(8,128)}, s32[3,8,128]{2,1,0:T(...) custom-call(s32[64]{0:T(128)} %counts.1, f32[3,64,128]{2,1,0:T(8,128)} %bitcast.9, ...), custom_call_target="tpu_custom_call" | custom-call | tf_op jit(solution)/shard_map/upward/pallas_call | solution.py:539
  52.3 2.5 %plan.1 = s32[288,128]{1,0:T(8,128)} custom-call(s32[1]{0:T(128)} %bitcast.first, s32[27,64]{1,0:T(8,128)} %bitcast.12, s32[3,8,128]{2,1,0:T(8,128)} %get-tuple-element.13.rows), custom_call_target="tpu_custom_call" | custom-call | tf_op jit(solution)/shard_map/plan/pallas_call | solution.py:126
  54.8 35.3 %near.1 = f32[64,32,128]{2,1,0:T(8,128)} custom-call(s32[36864]{0:T(1024)} %bitcast.8, f32[3,64,128]{2,1,0:T(8,128)} %get-tuple-element.14.p0, f32[3,64,128]{2,1,0:T(8,128)} %bitcast.10, f32[3,64,128]{2,1,0:T(8,128)} %get-tuple-element.15.p2, f32[64,32,128]{2,1,0:T(8,128)} %get-tuple-element.16.d0, f32[64,32,128]{2,1,0:T(8,128)} %d1.1, ...), custom_call_target="tpu_custom_call" | custom-call | tf_op jit(solution)/shard_map/near/pallas_call | solution.py:267

commit v8 on v7

--- a/solution.py
+++ b/solution.py
@@ -330,6 +330,7 @@
         copy.start()
         return copy
 
+    early, rest = pl.ds(0, leaves // 2), pl.ds(leaves // 2, leaves // 2)
     count_rows[1] = jnp.zeros((8, 128), jnp.int32)
     count_rows[1, :1, :leaves] = count_row[...]
     halo = [
@@ -337,6 +338,8 @@
         push(count_rows.at[1], count_rows.at[2], 29, left),
         push(pts, pts_lo, 0, right),
         push(pts, pts_hi, 1, left),
+        push(dens.at[early], dens_lo.at[early], 2, right),
+        push(dens.at[early], dens_hi.at[early], 3, left),
     ]
 
     surf_pad[...] = jnp.zeros_like(surf_pad)
@@ -431,7 +434,7 @@
             sources[slab, :, i, :] = turned[:width]
 
     turn(1)
-    for copy in halo[4:]:
+    for copy in halo[6:]:
         copy.wait_recv()
     turn(0)
     turn(2)
@@ -454,7 +457,10 @@
         top1 = top1 + near_top[k, :, :width]
     far_top[0, :, :width] = top1
     more = [push(far_top.at[0], far_top.at[k], 12 + k, cousins[k - 1]) for k in range(1, rows)]
-    late = [push(dens, dens_lo, 2, right), push(dens, dens_hi, 3, left)]
+    late = [
+        push(dens.at[rest], dens_lo.at[rest], 30, right),
+        push(dens.at[rest], dens_hi.at[rest], 31, left),
+    ]
     total = dot3(top1, coarse[child])
     lax.fori_loop(2, blocks // 2, far_pair, 0)
     for copy in more:
@@ -496,7 +502,7 @@
         return carry
 
     lax.fori_loop(0, 2, descend, 0)
-    for copy in halo[:4] + late:
+    for copy in halo[:6] + late:
         copy.wait_recv()
     for copy in halo + late + copies + more:
         copy.wait_send()
@@ -558,8 +564,8 @@
             pltpu.VMEM((3, leaves, 128), F32),
             pltpu.VMEM((256, 384), F32),
             pltpu.VMEM((vlist.shape[1], 256), BF),
-            pltpu.SemaphoreType.DMA((30,)),
-            pltpu.SemaphoreType.DMA((30,)),
+            pltpu.SemaphoreType.DMA((32,)),
+            pltpu.SemaphoreType.DMA((32,)),
             pltpu.SemaphoreType.DMA((width // STEP,)),
         ],
         compiler_params=pltpu.CompilerParams(

time: 90.3 us -> 84.2 us (0.932)
  Pallas kernels: 90 us -> 83.9 us
    pallas_call x1, Pallas kernels: 52.3 us -> 46.2 us  [up_call(): pl.pallas_call(up_kernel, out_shape=[like(pts.shape, F32), like(pts.shape...]
where the time goes in v8:
time: 84.2 us; the launch traced here: 83.9 us
  Pallas kernels  83.9 us (100%)
    pallas_call x1, Pallas kernels, up_call(): pl.pallas_call(up_kernel, out_shape=[like(pts.shape, F32), like(pts.shape...  46.2 us
    pallas_call x1, Pallas kernels, near_call(): pl.pallas_call(functools.partial(near_kernel, leaves), out_shape=jax.Shap...  35.2 us
    pallas_call x1, Pallas kernels, plan_call(): pl.pallas_call(functools.partial(plan_kernel, leaves), out_shape=jax.Shap...  2.5 us

profile of v8, /device:TPU:1, one launch (start us, length us, event | category | flops | bytes accessed | tf_op | source)
XLA Modules:
  0.0 83.9 jit_solution(11343808878612963485)
XLA Ops:
  0.0 46.2 %upward.1 = (f32[3,64,128]{2,1,0:T(8,128)}, f32[3,64,128]{2,1,0:T(8,128)}, f32[64,32,128]{2,1,0:T(8,128)}, f32[64,32,128]{2,1,0:T(8,128)}, s32[3,8,128]{2,1,0:T(...) custom-call(s32[64]{0:T(128)} %counts.1, f32[3,64,128]{2,1,0:T(8,128)} %bitcast.9, ...), custom_call_target="tpu_custom_call" | custom-call | tf_op jit(solution)/shard_map/upward/pallas_call | solution.py:545
  46.2 2.5 %plan.1 = s32[288,128]{1,0:T(8,128)} custom-call(s32[1]{0:T(128)} %bitcast.first, s32[27,64]{1,0:T(8,128)} %bitcast.12, s32[3,8,128]{2,1,0:T(8,128)} %get-tuple-element.13.rows), custom_call_target="tpu_custom_call" | custom-call | tf_op jit(solution)/shard_map/plan/pallas_call | solution.py:126
  48.7 35.2 %near.1 = f32[64,32,128]{2,1,0:T(8,128)} custom-call(s32[36864]{0:T(1024)} %bitcast.8, f32[3,64,128]{2,1,0:T(8,128)} %get-tuple-element.14.p0, f32[3,64,128]{2,1,0:T(8,128)} %bitcast.10, f32[3,64,128]{2,1,0:T(8,128)} %get-tuple-element.15.p2, f32[64,32,128]{2,1,0:T(8,128)} %get-tuple-element.16.d0, f32[64,32,128]{2,1,0:T(8,128)} %d1.1, ...), custom_call_target="tpu_custom_call" | custom-call | tf_op jit(solution)/shard_map/near/pallas_call | solution.py:267
